TPU v7x, 512 devices: a whole 4x8x8 slice. The times are simulated.
512 devices in a mesh: row: 32 (over y_lo, z, core), col: 16 (over y_hi, x).
Axes of the slice: x: 4, y: 8 (y_hi: 4, y_lo: 2; y = y_hi * 2 + y_lo), z: 8, core: 2. Of those that a mesh axis runs over, the one named last changes fastest.
Arguments:
- active_flags: int32 [256, 128], P('row', 'col'), may hold values 0 or 1
- port_index: int32 [256, 128], P('row', 'col'), may hold values from 0 to 7
- drive_weights: float32 [2, 4, 256, 128], P(None, None, 'row', 'col'), may hold values from -6 to 6
- feed_table: float32 [2, 8, 1024], replicated, may hold values from -6 to 6
- cell_map: bfloat16 [2, 1024, 1024], replicated, may hold values from -0.125 to 0.125
- probe_weights: float32 [2, 1024], replicated, may hold values from -0.1875 to 0.1875
Outputs:
- currents: float32 [2, 4, 256, 128], P(None, None, 'row', 'col')
- far_pattern: float32 [2, 4, 1024, 512], P(None, None, 'row', 'col')
All inputs are finite; a program needn't handle non-finite values. No bound on the sum of `active_flags` on one device may be relied on, other than what follows from the above.
Results may differ from a plain program's by a relative error of at most 0.0024.
Values sent between devices are 32-bit elements; how exact they have to be, the bound alone decides.
No kernel may reach another device: no remote copies, remote signals or barrier semaphores. Data moves between devices by JAX's collectives and lax.ppermute only.
A program may use at most 64 MiB of HBM per device.

v0:
```python
import math

import jax
import jax.numpy as jnp
from jax import lax
from jax.sharding import PartitionSpec as P

ITERS = 2
OVER = 4


relaxation = 0.75
reflect_re = -0.3
reflect_im = 0.2


def with_halo(value, sides, width):
    for axis, dim in sides:
        size, length = (lax.axis_size(axis), value.shape[dim])
        up = [(i, (i + 1) % size) for i in range(size - 1)]
        down = [(j, i) for i, j in up]
        last = lax.slice_in_dim(value, length - width, length, axis=dim)
        initial = lax.slice_in_dim(value, 0, width, axis=dim)
        before = lax.ppermute(last, axis, up)
        after = lax.ppermute(initial, axis, down)
        value = jnp.concatenate([before, value, after], axis=dim)
    return value


def reflect(edge_wave):
    return jnp.stack(
        [
            reflect_re * edge_wave[0] - reflect_im * edge_wave[1],
            reflect_re * edge_wave[1] + reflect_im * edge_wave[0],
        ]
    )


def apply_map(rounded, weights):
    layout = rounded.shape
    flattened = rounded.reshape(-1, layout[-1])
    real_part = jnp.dot(flattened, weights[0], preferred_element_type=jnp.float32).reshape(
        layout[:-1] + (weights.shape[2],)
    )
    imag_part = jnp.dot(flattened, weights[1], preferred_element_type=jnp.float32).reshape(
        layout[:-1] + (weights.shape[2],)
    )
    return jnp.stack([real_part[0] - imag_part[1], imag_part[0] + real_part[1]])


def twiddle(first_index, second_index, length):
    products = first_index[:, None] * second_index[None, :] % length
    angles = products.astype(jnp.float32) * (2.0 * math.pi / length)
    return (jnp.cos(angles), -jnp.sin(angles))


def along_columns(values, cos_table, sin_table):
    highest = lax.Precision.HIGHEST
    real_part = jnp.einsum("xsrc,ck->xsrk", values, cos_table, precision=highest)
    imag_part = jnp.einsum("xsrc,ck->xsrk", values, sin_table, precision=highest)
    return jnp.stack([real_part[0] - imag_part[1], imag_part[0] + real_part[1]])


def along_rows(values, cos_table, sin_table):
    highest = lax.Precision.HIGHEST
    real_part = jnp.einsum("xsrk,rl->xslk", values, cos_table, precision=highest)
    imag_part = jnp.einsum("xsrk,rl->xslk", values, sin_table, precision=highest)
    return jnp.stack([real_part[0] - imag_part[1], imag_part[0] + real_part[1]])


def fetch_far(outgoing, edge_size):
    padded = with_halo(outgoing, (("row", 2), ("col", 3)), 1)
    from_north = padded[:, :, 0, 1:-1, edge_size : 2 * edge_size]
    from_south = padded[:, :, -1, 1:-1, 0:edge_size]
    from_west = padded[:, :, 1:-1, 0, 3 * edge_size :]
    from_east = padded[:, :, 1:-1, -1, 2 * edge_size : 3 * edge_size]
    row_at = lax.axis_index("row")
    col_at = lax.axis_index("col")
    from_north = jnp.where(row_at == 0, reflect(outgoing[:, :, 0, :, 0:edge_size]), from_north)
    from_south = jnp.where(
        row_at == lax.axis_size("row") - 1,
        reflect(outgoing[:, :, -1, :, edge_size : 2 * edge_size]),
        from_south,
    )
    from_west = jnp.where(
        col_at == 0, reflect(outgoing[:, :, :, 0, 2 * edge_size : 3 * edge_size]), from_west
    )
    from_east = jnp.where(
        col_at == lax.axis_size("col") - 1,
        reflect(outgoing[:, :, :, -1, 3 * edge_size :]),
        from_east,
    )
    return (from_north, from_south, from_west, from_east)


def couple_block(outgoing, previous, far_traces):
    edge_size = outgoing.shape[-1] // 4
    from_north, from_south, from_west, from_east = far_traces
    north_in = jnp.concatenate(
        [from_north[:, :, None], outgoing[:, :, :-1, :, edge_size : 2 * edge_size]], axis=2
    )
    south_in = jnp.concatenate([outgoing[:, :, 1:, :, 0:edge_size], from_south[:, :, None]], axis=2)
    west_in = jnp.concatenate(
        [from_west[:, :, :, None], outgoing[:, :, :, :-1, 3 * edge_size :]], axis=3
    )
    east_in = jnp.concatenate(
        [outgoing[:, :, :, 1:, 2 * edge_size : 3 * edge_size], from_east[:, :, :, None]], axis=3
    )
    arrived = jnp.concatenate([north_in, south_in, west_in, east_in], axis=-1)
    return relaxation * arrived + (1.0 - relaxation) * previous


def advance(outgoing, previous, cell_map, source):
    edge_size = outgoing.shape[-1] // 4
    incoming = couple_block(outgoing, previous, fetch_far(outgoing, edge_size))
    return (incoming, apply_map(incoming.astype(jnp.bfloat16), cell_map) + source)


def body(active_flags, port_index, drive_weights, feed_table, cell_map, probe_weights):
    port_count = feed_table.shape[1]
    row_count = active_flags.shape[0]
    col_count = active_flags.shape[1]
    onehot = (
        port_index[:, :, None] == jnp.arange(port_count, dtype=jnp.int32)[None, None, :]
    ).astype(jnp.float32)
    feed_cells = jnp.einsum("rcp,xpu->xrcu", onehot, feed_table, precision=lax.Precision.HIGHEST)
    amplitude = drive_weights * active_flags.astype(jnp.float32)[None, None]
    amp_re = amplitude[0][..., None]
    amp_im = amplitude[1][..., None]
    source = jnp.stack(
        [
            amp_re * feed_cells[0][None] - amp_im * feed_cells[1][None],
            amp_re * feed_cells[1][None] + amp_im * feed_cells[0][None],
        ]
    )
    outgoing = source
    incoming = jnp.zeros_like(source)
    for iteration in range(ITERS):
        incoming, outgoing = advance(outgoing, incoming, cell_map, source)
    totals = outgoing + incoming
    currents = jnp.stack(
        [
            jnp.sum(probe_weights[0] * totals[0] - probe_weights[1] * totals[1], axis=-1),
            jnp.sum(probe_weights[0] * totals[1] + probe_weights[1] * totals[0], axis=-1),
        ]
    )
    total_rows = row_count * lax.axis_size("row")
    total_cols = col_count * lax.axis_size("col")
    span_x = OVER * total_rows
    span_y = OVER * total_cols
    col_first = lax.axis_index("col") * col_count
    cos_y, sin_y = twiddle(
        col_first + jnp.arange(col_count, dtype=jnp.int32),
        jnp.arange(span_y, dtype=jnp.int32),
        span_y,
    )
    section_one = lax.psum_scatter(
        along_columns(currents, cos_y, sin_y), "col", scatter_dimension=3, tiled=True
    )
    row_first = lax.axis_index("row") * row_count
    cos_x, sin_x = twiddle(
        row_first + jnp.arange(row_count, dtype=jnp.int32),
        jnp.arange(span_x, dtype=jnp.int32),
        span_x,
    )
    far_pattern = lax.psum_scatter(
        along_rows(section_one, cos_x, sin_x), "row", scatter_dimension=2, tiled=True
    )
    far_pattern = far_pattern * (total_rows * total_cols) ** (-0.5)
    return (currents, far_pattern)


def solution(mesh):
    placed = (P("row", "col"), P("row", "col"), P(None, None, "row", "col"), P(), P(), P())
    return jax.shard_map(
        body,
        mesh=mesh,
        in_specs=placed,
        out_specs=(P(None, None, "row", "col"), P(None, None, "row", "col")),
        check_vma=False,
    )
```

profile of v0, /device:TPU:6, one launch (start us, length us, event | category | flops | bytes accessed | tf_op | source)
XLA Modules:
  0.0 352.6 jit_solution(5322200003200586538)
XLA Ops:
  7.2 0.8 copy-done
  8.0 1.1 convolution_bitcast_fusion.2
  10.0 1.2 fusion.20
  11.2 1.3 collective-permute-start.1
  12.5 3.8 %collective-permute-start = (f32[2,4,1,8,1024]{4,2,3,1,0:T(1,128)}, f32[2,4,1,8,1024]{4,2,3,1,0:T(1,128)}, u32[]{:S(2)}, u32[]{:S(2)}) collective-permute-start(f32[2,4,1,8,1024]{4,2,3,1,0:T(1,128)} %get-tuple-element.50), channel_id=1, source_target_pairs={{0,16},{16,32},{32,48},{48,64},{64,80},{80,96},{96,112},{112,128},... | collective-permute-start | bytes 786440 | tf_op jit(solution)/shard_map/ppermute | solution.py:24
  16.4 0.6 multiply_subtract_fusion.6
  17.0 1.0 fusion.18
  18.3 1.0 pad_maximum_fusion.9
  19.3 2.7 collective-permute-start.3
  22.0 6.1 %collective-permute-start.2 = (f32[2,4,10,1,1024]{4,2,3,1,0:T(8,128)S(1)}, f32[2,4,10,1,1024]{4,2,3,1,0:T(8,128)S(1)}, u32[]{:S(2)}, u32[]{:S(2)}) collective-permute-start(f32[2,4,10,1,1024]{4,2,3,1,0:T(8,128)S(1)} %get-tuple-element.20), channel_id=1, source_target_pairs={{0,1},{1,2},{2,3},{3,4},{4,5},{5,6},{6,7},{7,8},{8,9},{9,10},{10,1... | collective-permute-start | bytes 983048 | tf_op jit(solution)/shard_map/ppermute | solution.py:24
  28.2 1.0 broadcast_select_fusion.3
  29.8 7.4 %collective-permute-done.3 = f32[2,4,10,1,1024]{4,2,3,1,0:T(8,128)S(1)} collective-permute-done((f32[2,4,10,1,1024]{4,2,3,1,0:T(8,128)S(1)}, f32[2,4,10,1,1024]{4,2,3,1,0:T(8,128)S(1)}, u32[]{:S(2)}, u32[]{:S(2)}) %collective-permute-start.3) | collective-permute-done | bytes 327712 | tf_op jit(solution)/shard_map/ppermute | solution.py:25
  37.2 1.7 collective-permute-done.2
  39.4 1.7 copy-done.9
  41.1 1.2 fusion.10
  42.3 1.3 fusion.6
  43.6 0.6 slice_subtract_fusion.1
  44.2 0.6 copy.40
  44.8 0.6 copy.41
  45.4 0.4 maximum_add_fusion
  45.8 0.4 fusion.72
  46.5 3.7 %collective-permute-start.4 = (f32[2,4,1,8,1024]{4,2,3,1,0:T(1,128)S(1)}, f32[2,4,1,8,1024]{4,2,3,1,0:T(1,128)S(1)}, u32[]{:S(2)}, u32[]{:S(2)}) collective-permute-start(f32[2,4,1,8,1024]{4,2,3,1,0:T(1,128)S(1)} %get-tuple-element.36), channel_id=1, source_target_pairs={{0,16},{16,32},{32,48},{48,64},{64,80},{80,96},{96,112},{112,128},... | collective-permute-start | bytes 786440 | tf_op jit(solution)/shard_map/ppermute | solution.py:24
  50.2 1.3 collective-permute-start.5
  52.0 15.1 %collective-permute-done.5 = f32[2,4,1,8,1024]{4,2,3,1,0:T(1,128)S(1)} collective-permute-done((f32[2,4,1,8,1024]{4,2,3,1,0:T(1,128)S(1)}, f32[2,4,1,8,1024]{4,2,3,1,0:T(1,128)S(1)}, u32[]{:S(2)}, u32[]{:S(2)}) %collective-permute-start.5) | collective-permute-done | bytes 262176 | tf_op jit(solution)/shard_map/ppermute | solution.py:25
  67.3 1.9 collective-permute-start.6
  69.6 4.1 %collective-permute-start.7 = (f32[2,4,10,1,1024]{4,2,3,1,0:T(8,128)S(1)}, f32[2,4,10,1,1024]{4,2,3,1,0:T(8,128)S(1)}, u32[]{:S(2)}, u32[]{:S(2)}) collective-permute-start(f32[2,4,10,1,1024]{4,2,3,1,0:T(8,128)S(1)} %get-tuple-element.19), channel_id=1, source_target_pairs={{1,0},{2,1},{3,2},{4,3},{5,4},{6,5},{7,6},{8,7},{9,8},{10,9},{11,1... | collective-permute-start | bytes 983048 | tf_op jit(solution)/shard_map/ppermute | solution.py:25
  73.7 6.4 %collective-permute-done.6 = f32[2,4,10,1,1024]{4,2,3,1,0:T(8,128)S(1)} collective-permute-done((f32[2,4,10,1,1024]{4,2,3,1,0:T(8,128)S(1)}, f32[2,4,10,1,1024]{4,2,3,1,0:T(8,128)S(1)}, u32[]{:S(2)}, u32[]{:S(2)}) %collective-permute-start.6) | collective-permute-done | bytes 327712 | tf_op jit(solution)/shard_map/ppermute | solution.py:24
  80.4 5.1 %collective-permute-done.7 = f32[2,4,10,1,1024]{4,2,3,1,0:T(8,128)S(1)} collective-permute-done((f32[2,4,10,1,1024]{4,2,3,1,0:T(8,128)S(1)}, f32[2,4,10,1,1024]{4,2,3,1,0:T(8,128)S(1)}, u32[]{:S(2)}, u32[]{:S(2)}) %collective-permute-start.7) | collective-permute-done | bytes 327712 | tf_op jit(solution)/shard_map/ppermute | solution.py:25
  86.0 1.3 fusion.4
  87.2 1.3 fusion.8
  88.5 0.4 slice_subtract_fusion
  88.9 0.6 copy.46
  89.5 0.6 copy.47
  90.1 1.0 fusion.2
  91.1 0.4 subtract_reduce_fusion
  91.7 0.4 fusion.41
  92.0 0.4 fusion.39
  92.5 1.1 copy.56
  93.5 2.0 reshape.340
  95.6 117.7 %reduce-scatter.7.cloned.1.call-done = f32[32,64]{1,0:T(8,128)} async-done(((f32[512,64]{1,0:T(8,128)}), f32[32,64]{1,0:T(8,128)}) %reduce-scatter.7.cloned.1.call-update) | async-done | bytes 8208
  213.3 0.8 reshape.341
  214.2 1.1 convolution_bitcast_fusion.1
  215.4 1.1 convolution_bitcast_fusion
  216.8 3.1 copy.58
  219.9 5.0 %reshape.342 = f32[1024,256]{1,0:T(8,128)} reshape(f32[1024,2,4,32]{3,2,1,0:T(4,128)} %bitcast.91) | data formatting | bytes 2097152
  224.9 119.1 %reduce-scatter.9.cloned.1.call-done = f32[32,256]{1,0:T(8,128)} async-done(((f32[1024,256]{1,0:T(8,128)}), f32[32,256]{1,0:T(8,128)}) %reduce-scatter.9.cloned.1.call-update) | async-done | bytes 32784
  344.0 0.9 reshape.343
  345.0 0.8 copy.50
  (76 shorter events, 5.1 us)
Async XLA Ops:
  7.2 0.8 copy-start
  7.2 2.3 copy-start.8
  7.2 2.3 copy-start.6
  7.2 206.1 %reduce-scatter.7.cloned.1.call-start = ((), (), s32[]{:S(2)}) async-start(), calls=%async_computation.2 | async-start | bytes 278528
  11.2 7.1 %collective-permute-start.1 = (f32[2,4,1,8,1024]{4,2,3,1,0:T(1,128)}, f32[2,4,1,8,1024]{4,2,3,1,0:T(1,128)S(1)}, u32[]{:S(2)}, u32[]{:S(2)}) collective-permute-start(f32[2,4,1,8,1024]{4,2,3,1,0:T(1,128)} %get-tuple-element.51), channel_id=1, source_target_pairs={{16,0},{32,16},{48,32},{64,48},{80,64},{96,80},{112,96},{128,112},... | collective-permute-start | bytes 786440 | tf_op jit(solution)/shard_map/ppermute | solution.py:25
  12.5 5.8 %collective-permute-start = (f32[2,4,1,8,1024]{4,2,3,1,0:T(1,128)}, f32[2,4,1,8,1024]{4,2,3,1,0:T(1,128)}, u32[]{:S(2)}, u32[]{:S(2)}) collective-permute-start(f32[2,4,1,8,1024]{4,2,3,1,0:T(1,128)} %get-tuple-element.50), channel_id=1, source_target_pairs={{0,16},{16,32},{32,48},{48,64},{64,80},{80,96},{96,112},{112,128},... | collective-permute-start | bytes 786440 | tf_op jit(solution)/shard_map/ppermute | solution.py:24
  16.4 1.7 copy-start.7
  19.3 17.9 %collective-permute-start.3 = (f32[2,4,10,1,1024]{4,2,3,1,0:T(8,128)S(1)}, f32[2,4,10,1,1024]{4,2,3,1,0:T(8,128)S(1)}, u32[]{:S(2)}, u32[]{:S(2)}) collective-permute-start(f32[2,4,10,1,1024]{4,2,3,1,0:T(8,128)S(1)} %get-tuple-element.21), channel_id=1, source_target_pairs={{1,0},{2,1},{3,2},{4,3},{5,4},{6,5},{7,6},{8,7},{9,8},{10,9},{11,1... | collective-permute-start | bytes 983048 | tf_op jit(solution)/shard_map/ppermute | solution.py:25
  22.0 16.8 %collective-permute-start.2 = (f32[2,4,10,1,1024]{4,2,3,1,0:T(8,128)S(1)}, f32[2,4,10,1,1024]{4,2,3,1,0:T(8,128)S(1)}, u32[]{:S(2)}, u32[]{:S(2)}) collective-permute-start(f32[2,4,10,1,1024]{4,2,3,1,0:T(8,128)S(1)} %get-tuple-element.20), channel_id=1, source_target_pairs={{0,1},{1,2},{2,3},{3,4},{4,5},{5,6},{6,7},{7,8},{8,9},{9,10},{10,1... | collective-permute-start | bytes 983048 | tf_op jit(solution)/shard_map/ppermute | solution.py:24
  29.2 8.0 %copy-start.4 = (f32[1,4,8,1,256]{4,2,3,1,0:T(8,128)S(1)}, f32[1,4,8,1,256]{4,2,3,1,0:T(8,128)}, u32[]{:S(2)}) copy-start(f32[1,4,8,1,256]{4,2,3,1,0:T(8,128)} %get-tuple-element.46) | copy-start | bytes 98308
  29.2 8.0 %copy-start.5 = (f32[1,4,8,1,256]{4,2,3,1,0:T(8,128)S(1)}, f32[1,4,8,1,256]{4,2,3,1,0:T(8,128)}, u32[]{:S(2)}) copy-start(f32[1,4,8,1,256]{4,2,3,1,0:T(8,128)} %get-tuple-element.47) | copy-start | bytes 98308
  29.2 9.6 %copy-start.1 = (f32[2,4,8,7,256]{4,2,3,1,0:T(8,128)S(1)}, f32[2,4,8,7,256]{4,2,3,1,0:T(8,128)}, u32[]{:S(2)}) copy-start(f32[2,4,8,7,256]{4,2,3,1,0:T(8,128)} %get-tuple-element.48) | copy-start | bytes 1376260
  29.2 9.6 %copy-start.2 = (f32[2,4,8,7,256]{4,2,3,1,0:T(8,128)S(1)}, f32[2,4,8,7,256]{4,2,3,1,0:T(8,128)}, u32[]{:S(2)}) copy-start(f32[2,4,8,7,256]{4,2,3,1,0:T(8,128)} %get-tuple-element.49) | copy-start | bytes 1376260
  38.9 2.2 copy-start.9
  46.5 5.1 %collective-permute-start.4 = (f32[2,4,1,8,1024]{4,2,3,1,0:T(1,128)S(1)}, f32[2,4,1,8,1024]{4,2,3,1,0:T(1,128)S(1)}, u32[]{:S(2)}, u32[]{:S(2)}) collective-permute-start(f32[2,4,1,8,1024]{4,2,3,1,0:T(1,128)S(1)} %get-tuple-element.36), channel_id=1, source_target_pairs={{0,16},{16,32},{32,48},{48,64},{64,80},{80,96},{96,112},{112,128},... | collective-permute-start | bytes 786440 | tf_op jit(solution)/shard_map/ppermute | solution.py:24
  50.2 16.9 %collective-permute-start.5 = (f32[2,4,1,8,1024]{4,2,3,1,0:T(1,128)S(1)}, f32[2,4,1,8,1024]{4,2,3,1,0:T(1,128)S(1)}, u32[]{:S(2)}, u32[]{:S(2)}) collective-permute-start(f32[2,4,1,8,1024]{4,2,3,1,0:T(1,128)S(1)} %get-tuple-element.37), channel_id=1, source_target_pairs={{16,0},{32,16},{48,32},{64,48},{80,64},{96,80},{112,96},{128,112},... | collective-permute-start | bytes 786440 | tf_op jit(solution)/shard_map/ppermute | solution.py:25
  67.3 12.8 %collective-permute-start.6 = (f32[2,4,10,1,1024]{4,2,3,1,0:T(8,128)S(1)}, f32[2,4,10,1,1024]{4,2,3,1,0:T(8,128)S(1)}, u32[]{:S(2)}, u32[]{:S(2)}) collective-permute-start(f32[2,4,10,1,1024]{4,2,3,1,0:T(8,128)S(1)} %get-tuple-element.18), channel_id=1, source_target_pairs={{0,1},{1,2},{2,3},{3,4},{4,5},{5,6},{6,7},{7,8},{8,9},{9,10},{10,1... | collective-permute-start | bytes 983048 | tf_op jit(solution)/shard_map/ppermute | solution.py:24
  69.6 15.8 %collective-permute-start.7 = (f32[2,4,10,1,1024]{4,2,3,1,0:T(8,128)S(1)}, f32[2,4,10,1,1024]{4,2,3,1,0:T(8,128)S(1)}, u32[]{:S(2)}, u32[]{:S(2)}) collective-permute-start(f32[2,4,10,1,1024]{4,2,3,1,0:T(8,128)S(1)} %get-tuple-element.19), channel_id=1, source_target_pairs={{1,0},{2,1},{3,2},{4,3},{5,4},{6,5},{7,6},{8,7},{9,8},{10,9},{11,1... | collective-permute-start | bytes 983048 | tf_op jit(solution)/shard_map/ppermute | solution.py:25
  91.7 3.9 %copy-start.3 = (f32[2,4,8,8]{3,2,1,0:T(8,128)}, f32[2,4,8,8]{3,2,1,0:T(8,128)S(1)}, u32[]{:S(2)}) copy-start(f32[2,4,8,8]{3,2,1,0:T(8,128)S(1)} %pad_maximum_fusion.19) | copy-start | bytes 6148
  95.6 248.4 %reduce-scatter.9.cloned.1.call-start = ((), (), s32[]{:S(2)}) async-start(), calls=%async_computation.3 | async-start | bytes 1081344
Sparse Core Ops, SparseCore 0:
  95.7 117.5 reduce-scatter.6
  225.0 118.8 reduce-scatter.8
where the time goes:
time: 353 us
  waiting for transfers between devices  272 us (77%)
  starting transfers between devices  24.9 us (7%)
  local copies, waits for them, and re-layouts  21.3 us (6%)
  between operations  14.7 us (4%)
  other arithmetic  10.1 us (3%)
  matrix products  9.1 us (3%)
    unnamed x4, waiting for transfers between devices  237 us
    ppermute x4, waiting for transfers between devices, with_halo(): after = lax.ppermute(initial, axis, down)  27.5 us
    unnamed x29, local copies, waits for them, and re-layouts  16.3 us
    ppermute x4, starting transfers between devices, with_halo(): before = lax.ppermute(last, axis, up)  15.5 us
    ppermute x4, starting transfers between devices, with_halo(): after = lax.ppermute(initial, axis, down)  9.41 us
    ppermute x4, waiting for transfers between devices, with_halo(): before = lax.ppermute(last, axis, up)  8.08 us
  transfers between devices with their start and end apart: 10, of which 7 were waited for; matrix products, arithmetic and copies ran while one was open for 1% of the time, Pallas kernels for 0%

commit v1 on v0

v1 whole, which is shorter than its diff:
```python
import functools
import math

import jax
import jax.numpy as jnp
import numpy as np
from jax import lax
from jax.experimental import pallas as pl
from jax.experimental.pallas import tpu as pltpu
from jax.sharding import PartitionSpec as P

OVER = 4
PORTS = 8
STATES = 4
BLOCK = 8
REACH = 2
WIDE = 12
LANES = 128

relaxation = 0.75
reflect_re = -0.3
reflect_im = 0.2

STEP = ((-1, 0), (1, 0), (0, -1), (0, 1))
PLACES = tuple(
    (dr, dc) for dr in range(-2, 3) for dc in range(-2, 3) if abs(dr) + abs(dc) <= 2
)
CLASSES = 13
ROWS = 32


def path_matrix():
    twice = relaxation * relaxation
    once = relaxation * (1.0 - relaxation) + relaxation
    mix = np.zeros((CLASSES * ROWS, 18 * 24), np.float32)

    def add(weight, first, second, place, kind):
        d = PLACES.index(place)
        for part, left, right, sign in ((0, 0, 0, 1), (0, 1, 1, -1), (1, 0, 1, 1), (1, 1, 0, 1)):
            at = 16 + right if second is None else right * 8 + second
            mix[kind * ROWS + part * 13 + d, (first * 2 + left) * 24 + at] += sign * weight

    def corner(e, f):
        return 9 + (min(e, f) % 2) * 2 + (max(e, f) % 2)

    add(1.0, 0, None, (0, 0), 0)
    for e in range(4):
        add(once, 0, e, STEP[e], 0)
        add(once, 0, 4 + e, (0, 0), 1 + e)
        for f in range(4):
            both = (STEP[e][0] + STEP[f][0], STEP[e][1] + STEP[f][1])
            crossed = e // 2 != f // 2
            add(twice, 1 + e, f, both, 0)
            if f == e ^ 1:
                add(-twice, 1 + e, f, both, 1 + e)
            if f != e:
                add(twice, 5 + e, f, STEP[f], 1 + e)
            if f == e:
                add(twice, 1 + e, 4 + f, STEP[e], 5 + e)
                add(twice, 5 + e, 4 + f, (0, 0), 1 + e)
            elif crossed:
                add(twice, 1 + e, 4 + f, STEP[e], 1 + f)
                add(twice, 5 + e, 4 + f, (0, 0), corner(e, f))
    return mix


def halves(value):
    high = value.astype(jnp.bfloat16)
    return high, (value - high.astype(jnp.float32)).astype(jnp.bfloat16)


def cosine(turns, length):
    centred = jnp.where(turns >= length // 2, length - turns, turns)
    angle = (length // 4 - centred).astype(jnp.float32) * (2.0 * math.pi / length)
    square = angle * angle
    value = 1.0 / 6227020800.0
    value = value * square - 1.0 / 39916800.0
    value = value * square + 1.0 / 362880.0
    value = value * square - 1.0 / 5040.0
    value = value * square + 1.0 / 120.0
    value = value * square - 1.0 / 6.0
    return angle + angle * square * value


def dot(left, right, dims=((1,), (0,))):
    return lax.dot_general(left, right, (dims, ((), ())), preferred_element_type=jnp.float32)


def dot3(left, right):
    high, low = left
    high_right, low_right = right
    return dot(high, high_right) + (dot(low, high_right) + dot(high, low_right))


def pack_kernel(drive_ref, flag_ref, port_ref, out_ref):
    active = flag_ref[...].astype(jnp.float32)
    pieces = [drive_ref[x, s] * active for x in range(2) for s in range(STATES)]
    pieces.append(port_ref[...].astype(jnp.float32))
    pieces.append(jnp.zeros((BLOCK, LANES - 9 * BLOCK), jnp.float32))
    packed = jnp.concatenate(pieces, axis=1)
    out_ref[...] = jnp.broadcast_to(packed[None], out_ref.shape)


def table_kernel(place, rows, cols, feed_ref, map_ref, probe_ref, mix_ref, table_ref, row_high_ref, row_low_ref, col_high_ref, col_low_ref, hops_ref):
    row_at, col_at = place()
    edge = feed_ref.shape[2] // 4
    units = 4 * edge

    def block(value, e):
        return value[:, e * edge : (e + 1) * edge]

    feed_re, feed_im = feed_ref[0], feed_ref[1]
    back_re = reflect_re * feed_re - reflect_im * feed_im
    back_im = reflect_re * feed_im + reflect_im * feed_re
    hops_ref[0:8, :] = feed_re
    hops_ref[8:16, :] = feed_im
    for a in range(4):
        e = a ^ 1
        enter = jnp.concatenate(
            [block(feed_re, e), block(feed_im, e), block(back_re, a), block(back_im, a)], axis=0
        )
        enter = jnp.concatenate(halves(enter), axis=0)
        by_re = dot(enter, map_ref[0, a * edge : (a + 1) * edge, :])
        by_im = dot(enter, map_ref[1, a * edge : (a + 1) * edge, :])
        by_re = by_re[0:32] + by_re[32:64]
        by_im = by_im[0:32] + by_im[32:64]
        for first, at in ((1 + e, 0), (5 + a, 16)):
            hops_ref[first * 16 : first * 16 + 8, :] = by_re[at : at + 8] - by_im[at + 8 : at + 16]
            hops_ref[first * 16 + 8 : first * 16 + 16, :] = (
                by_re[at + 8 : at + 16] + by_im[at : at + 8]
            )
    probe_re, probe_im = probe_ref[0:1, :], probe_ref[1:2, :]
    probes = jnp.concatenate(halves(jnp.concatenate([probe_re, probe_im] + [probe_re] * 6, axis=0)), axis=0)
    through_re = dot(probes, map_ref[0], ((1,), (1,)))
    through_im = dot(probes, map_ref[1], ((1,), (1,)))
    through_re = through_re[0:8] + through_re[8:16]
    through_im = through_im[0:8] + through_im[8:16]
    total_re = probe_re + through_re[0:1] - through_im[1:2]
    total_im = probe_im + through_im[0:1] + through_re[1:2]

    def swapped(value):
        return jnp.concatenate([block(value, e ^ 1) for e in range(4)], axis=1)

    sub = lax.broadcasted_iota(jnp.int32, (8, units), 0)
    lane = lax.broadcasted_iota(jnp.int32, (8, units), 1)
    own = lane // edge == sub % 4
    passed = sub < 4
    out_re = jnp.where(passed, swapped(total_re), reflect_re * total_re - reflect_im * total_im)
    out_im = jnp.where(passed, swapped(total_im), reflect_re * total_im + reflect_im * total_re)
    leave = jnp.concatenate(
        [
            jnp.where(own, out_re, 0.0),
            jnp.where(own, out_im, 0.0),
            jnp.where(sub == 0, probe_re, jnp.where(sub == 1, probe_im, 0.0)),
        ],
        axis=0,
    )
    products = lax.dot_general(
        leave, hops_ref[...], (((1,), (1,)), ((), ())),
        precision=lax.Precision.HIGHEST, preferred_element_type=jnp.float32,
    )
    flat = jnp.concatenate([products[:, 8 * k : 8 * k + 8] for k in range(18)], axis=0)
    table = lax.dot_general(
        mix_ref[...], flat, (((1,), (0,)), ((), ())),
        precision=lax.Precision.HIGHEST, preferred_element_type=jnp.float32,
    )
    wide = [table[k * ROWS : (k + 1) * ROWS, :] for k in range(CLASSES)]
    wide.append(jnp.zeros((ROWS, LANES - 8 * CLASSES), jnp.float32))
    table_ref[...] = jnp.concatenate(halves(jnp.concatenate(wide, axis=1)), axis=0)

    span = OVER * rows
    r = lax.broadcasted_iota(jnp.int32, (rows, LANES), 0)
    k = lax.broadcasted_iota(jnp.int32, (rows, LANES), 1)
    samples = OVER * BLOCK
    turns = (r * (row_at * samples + k)) & (span - 1)
    cos = jnp.where(k < samples, cosine(turns, span), 0.0)
    sin = jnp.where(k < samples, cosine((turns - span // 4) & (span - 1), span), 0.0)
    pick = (k >= samples) & (k < samples + BLOCK) & (r == row_at * BLOCK + k - samples)
    pick = jnp.where(pick, 1.0, 0.0)
    turn = jnp.concatenate(
        [
            jnp.concatenate([cos + pick, -sin], axis=1),
            jnp.concatenate([sin, cos + pick], axis=1),
        ],
        axis=0,
    )
    row_high_ref[...], row_low_ref[...] = halves(turn)

    span = OVER * cols
    shape = (samples, 2 * cols)
    q = lax.broadcasted_iota(jnp.int32, shape, 0) + col_at * samples
    k = lax.broadcasted_iota(jnp.int32, shape, 1)
    c = (k // 16) * BLOCK + k % 16 - REACH
    inside = (k % 16 < WIDE) & (c >= 0) & (c < cols)
    turns = (q * c) & (span - 1)
    scale = (rows * cols) ** -0.5
    cos = jnp.where(inside, cosine(turns, span) * scale, 0.0)
    sin = jnp.where(inside, cosine((turns - span // 4) & (span - 1), span) * scale, 0.0)
    turn = jnp.concatenate(
        [jnp.concatenate([cos, sin], axis=1), jnp.concatenate([-sin, cos], axis=1)], axis=0
    )
    col_high_ref[...], col_low_ref[...] = halves(turn)


def stencil_kernel(place, rows, cols, cells_ref, table_ref, row_high_ref, row_low_ref, out_ref, own_ref, coef_ref):
    _, col_at = place()
    across = cells_ref[...].T
    amps = [[across[(x * 4 + s) * 8 : (x * 4 + s) * 8 + 8] for s in range(STATES)] for x in range(2)]
    ports = across[64:72]

    sub = lax.broadcasted_iota(jnp.int32, (8, rows), 0).astype(jnp.float32)
    r = lax.broadcasted_iota(jnp.int32, (8, rows), 1)

    def flag(mask):
        return jnp.where(mask, 1.0, 0.0)

    north, south, north2, south2 = flag(r == 0), flag(r == rows - 1), flag(r == 1), flag(r == rows - 2)
    table = table_ref[...]
    for j in range(BLOCK):
        c = col_at * BLOCK + j
        west, east = flag(c == 0), flag(c == cols - 1)
        west2, east2 = flag(c == 1), flag(c == cols - 2)
        chosen = flag(jnp.broadcast_to(ports[j : j + 1], (8, rows)) == sub)
        at_north, at_south = chosen * north, chosen * south
        kinds = [
            chosen, at_north, at_south, chosen * west, chosen * east,
            chosen * north2, chosen * south2, chosen * west2, chosen * east2,
            at_north * west, at_north * east, at_south * west, at_south * east,
            jnp.zeros((LANES - 8 * CLASSES, rows), jnp.float32),
        ]
        found = dot(table, jnp.concatenate(kinds, axis=0).astype(jnp.bfloat16))
        found = found[0:ROWS] + found[ROWS : 2 * ROWS]
        for half in range(rows // LANES):
            coef_ref[half, j * ROWS : (j + 1) * ROWS, :] = found[:, half * LANES : (half + 1) * LANES]

    def coef(index):
        return jnp.concatenate(
            [coef_ref[half, pl.ds(index, 8, stride=ROWS), :] for half in range(rows // LANES)], axis=1
        )

    def moved(value, dr):
        if dr == 0:
            return value
        value = pltpu.roll(value, dr % rows, axis=1)
        return jnp.where(r >= dr if dr > 0 else r < rows + dr, value, 0.0)

    sums = {}
    for d, (dr, dc) in enumerate(PLACES):
        k_re, k_im = coef(d), coef(13 + d)
        for s in range(STATES):
            a_re, a_im = amps[0][s], amps[1][s]
            for x, value in ((0, k_re * a_re - k_im * a_im), (1, k_re * a_im + k_im * a_re)):
                value = moved(value, dr)
                key = (dc, s, x)
                sums[key] = sums[key] + value if key in sums else value

    spread = jnp.concatenate(
        [
            jnp.concatenate([sums[dc, s, 0], sums[dc, s, 1]], axis=1)
            for dc in range(-2, 3)
            for s in range(STATES)
        ],
        axis=0,
    )
    turned = dot3(halves(spread), (row_high_ref[...], row_low_ref[...]))
    samples = OVER * BLOCK
    lane = lax.broadcasted_iota(jnp.int32, (8, LANES), 1)
    first, second = lane < samples, (lane >= samples) & (lane < samples + BLOCK)
    nothing = jnp.zeros((16, LANES), jnp.float32)
    for x in range(2):
        main, near = nothing, nothing
        for i, dc in enumerate(range(-2, 3)):
            wave, own = jnp.zeros((8, LANES), jnp.float32), jnp.zeros((8, LANES), jnp.float32)
            for s in range(STATES):
                part = turned[(i * STATES + s) * 8 : (i * STATES + s) * 8 + 8, x * LANES : (x + 1) * LANES]
                a, b = jnp.where(first, part, 0.0), jnp.where(second, part, 0.0)
                wave = wave + (pltpu.roll(a, s * samples, axis=1) if s else a)
                own = own + pltpu.roll(b, (s - 1) * samples % LANES, axis=1) if s != 1 else own + b
            for_main = jnp.concatenate([wave, jnp.zeros((8, LANES), jnp.float32)], axis=0)
            for_near = jnp.concatenate([own, jnp.zeros((8, LANES), jnp.float32)], axis=0)
            shift = REACH + dc
            main = main + (pltpu.roll(for_main, shift, axis=0) if shift else for_main)
            near = near + (pltpu.roll(for_near, shift, axis=0) if shift else for_near)
        piece = jnp.concatenate([main[0:12], near[0:2], near[10:12]], axis=0)
        out_ref[:, :, x * LANES : (x + 1) * LANES] = jnp.broadcast_to(piece[None], (out_ref.shape[0], 16, LANES))
        own_ref[:, x * LANES : (x + 1) * LANES] = near


def pattern_kernel(place, blocks, got_ref, own_ref, col_high_ref, col_low_ref, currents_ref, far_ref):
    _, col_at = place()
    samples = OVER * BLOCK
    got = jnp.concatenate(
        [got_ref[:, :, x * LANES : (x + 1) * LANES].reshape(blocks * 16, LANES) for x in range(2)], axis=0
    )
    far = dot3((col_high_ref[...], col_low_ref[...]), halves(got))
    far = jnp.concatenate([far, jnp.zeros_like(far)], axis=0).T
    for x in range(2):
        for s in range(STATES):
            far_ref[x, s] = far[s * samples : (s + 1) * samples, x * samples : (x + 1) * samples]
    left, right = jnp.maximum(col_at - 1, 0), jnp.minimum(col_at + 1, blocks - 1)
    from_left = jnp.where(col_at > 0, 1.0, 0.0) * got_ref[left]
    from_right = jnp.where(col_at < blocks - 1, 1.0, 0.0) * got_ref[right]
    own = own_ref[...]
    whole = jnp.concatenate(
        [own[2:4] + from_left[14:16], own[4:8], own[8:10] + from_right[12:14]], axis=0
    )
    for x in range(2):
        flat = jnp.concatenate([whole[:, x * LANES : (x + 1) * LANES], jnp.zeros((LANES - 8, LANES), jnp.float32)], axis=0).T
        for s in range(STATES):
            currents_ref[x, s] = flat[s * samples : s * samples + BLOCK, 0:BLOCK]


def spot():
    return lax.axis_index("row"), lax.axis_index("col")


def call(kernel, out_shape, scratch=(), flops=0, size=0, **options):
    return pl.pallas_call(
        kernel,
        out_shape=out_shape,
        scratch_shapes=list(scratch),
        compiler_params=pltpu.CompilerParams(vmem_limit_bytes=40 * 1024 * 1024),
        cost_estimate=pl.CostEstimate(flops=flops, bytes_accessed=size, transcendentals=0),
        **options,
    )


def body(row_blocks, col_blocks, place, active_flags, port_index, drive_weights, feed_table, cell_map, probe_weights):
    rows, cols = row_blocks * BLOCK, col_blocks * BLOCK
    samples = OVER * BLOCK
    f32, b16 = jnp.float32, jnp.bfloat16
    shape = jax.ShapeDtypeStruct
    packed = call(pack_kernel, shape((row_blocks, BLOCK, LANES), f32), name="pack")(
        drive_weights, active_flags, port_index
    )
    cells = lax.all_to_all(packed, "row", 0, 0).reshape(rows, LANES)
    table, row_high, row_low, col_high, col_low = call(
        functools.partial(table_kernel, place, rows, cols),
        (
            shape((2 * ROWS, LANES), b16),
            shape((2 * rows, 2 * LANES), b16),
            shape((2 * rows, 2 * LANES), b16),
            shape((2 * samples, 4 * cols), b16),
            shape((2 * samples, 4 * cols), b16),
        ),
        scratch=[pltpu.VMEM((144, cell_map.shape[1]), f32)],
        flops=2 * 80 * 2 * 1024 * 1024,
        size=5 * 1024 * 1024,
        name="tables",
    )(feed_table, cell_map, probe_weights, jnp.asarray(path_matrix()))
    pieces, own = call(
        functools.partial(stencil_kernel, place, rows, cols),
        (shape((col_blocks, 16, 2 * LANES), f32), shape((16, 2 * LANES), f32)),
        scratch=[pltpu.VMEM((rows // LANES, BLOCK * ROWS, LANES), f32)],
        name="stencil",
    )(cells, table, row_high, row_low)
    got = lax.all_to_all(pieces, "col", 0, 0)
    return call(
        functools.partial(pattern_kernel, place, col_blocks),
        (shape((2, STATES, BLOCK, BLOCK), f32), shape((2, STATES, samples, samples), f32)),
        name="pattern",
    )(got, own, col_high, col_low)


def solution(mesh):
    placed = (P("row", "col"), P("row", "col"), P(None, None, "row", "col"), P(), P(), P())
    return jax.shard_map(
        functools.partial(body, mesh.shape["row"], mesh.shape["col"], spot),
        mesh=mesh,
        in_specs=placed,
        out_specs=(P(None, None, "row", "col"), P(None, None, "row", "col")),
        check_vma=False,
    )
```

time: 353 us -> 48.8 us (0.14)
  the two profiles are of different devices: /device:TPU:6 before, /device:TPU:8 now
where the time goes in v1:
time: 48.8 us; the launch traced here: 48.3 us
  blocking collectives  21.3 us (44%)
  starting transfers between devices  11.9 us (24%)
  Pallas kernels  7.37 us (15%)
  local copies, waits for them, and re-layouts  7 us (14%)
  between operations  0.68 us (1%)
    all_to_all x1, blocking collectives, body(): got = lax.all_to_all(pieces, 'col', 0, 0)  21.3 us
    all_to_all x1, starting transfers between devices, body(): cells = lax.all_to_all(packed, 'row', 0, 0).reshape(rows, LANES)  11.9 us
    unnamed x14, local copies, waits for them, and re-layouts  7 us
    pallas_call x1, Pallas kernels, body(): call(functools.partial(table_kernel, place, rows, cols), (shape((2 * ROWS...  4.69 us
    pallas_call x1, Pallas kernels, body(): call(functools.partial(pattern_kernel, place, col_blocks), (shape((2, STA...  1.03 us
  transfers between devices with their start and end apart: 1, of which 0 were waited for; matrix products, arithmetic and copies ran while one was open for 0% of the time, Pallas kernels for 10%

profile of v1, /device:TPU:8, one launch (start us, length us, event | category | flops | bytes accessed | tf_op | source)
XLA Modules:
  0.0 48.3 jit_solution(2349019886588075546)
XLA Ops:
  0.6 0.0 copy-start.3
  0.6 0.7 %copy-done.3 = f32[2,4,8,8]{3,2,1,0:T(8,128)S(1)} copy-done((f32[2,4,8,8]{3,2,1,0:T(8,128)S(1)}, f32[2,4,8,8]{3,2,1,0:T(8,128)}, u32[]{:S(2)}) %copy-start.3) | copy-done | bytes 2072
  1.4 0.0 copy-start.5
  1.4 0.7 %copy-done.5 = s32[8,8]{1,0:T(8,128)S(1)} copy-done((s32[8,8]{1,0:T(8,128)S(1)}, s32[8,8]{1,0:T(8,128)}, u32[]{:S(2)}) %copy-start.5) | copy-done | bytes 280
  2.1 0.0 copy-start.6
  2.1 0.7 %copy-done.6 = s32[8,8]{1,0:T(8,128)S(1)} copy-done((s32[8,8]{1,0:T(8,128)S(1)}, s32[8,8]{1,0:T(8,128)}, u32[]{:S(2)}) %copy-start.6) | copy-done | bytes 280
  2.8 0.7 %pack.1 = f32[32,8,128]{2,1,0:T(8,128)} custom-call(f32[2,4,8,8]{3,2,1,0:T(8,128)S(1)} %copy-done.3, s32[8,8]{1,0:T(8,128)S(1)} %copy-done.5, s32[8,8]{1,0:T(8,128)S(1)} %copy-done.6), custom_call_target="tpu_custom_call" | custom-call | tf_op jit(solution)/shard_map/pack/pallas_call | solution.py:333
  3.5 11.9 %all-to-all-start = ((f32[32,8,128]{2,1,0:T(8,128)}), f32[32,8,128]{2,1,0:T(8,128)S(1)}, u32[]{:S(2)}, u32[]{:S(2)}) async-start(f32[32,8,128]{2,1,0:T(8,128)} %pack.1), calls=%async_computation | async-start | bytes 262144 | tf_op jit(solution)/shard_map/all_to_all | solution.py:336
  15.5 0.0 copy-start
  15.5 2.2 %copy-done = bf16[2,1024,1024]{2,1,0:T(8,128)(2,1)S(1)} copy-done((bf16[2,1024,1024]{2,1,0:T(8,128)(2,1)S(1)}, bf16[2,1024,1024]{2,1,0:T(8,128)(2,1)}, u32[]{:S(2)}) %copy-start) | copy-done | bytes 4194328
  17.6 0.0 copy-start.1
  17.6 1.2 %copy-done.1 = f32[416,432]{1,0:T(8,128)S(1)} copy-done((f32[416,432]{1,0:T(8,128)S(1)}, f32[416,432]{1,0:T(8,128)}, u32[]{:S(2)}) %copy-start.1) | copy-done | bytes 718872
  18.8 0.0 copy-start.2
  18.8 0.8 %copy-done.2 = f32[2,8,1024]{2,1,0:T(8,128)S(1)} copy-done((f32[2,8,1024]{2,1,0:T(8,128)S(1)}, f32[2,8,1024]{2,1,0:T(8,128)}, u32[]{:S(2)}) %copy-start.2) | copy-done | bytes 65560
  19.6 0.0 copy-start.4
  19.6 0.7 %copy-done.4 = f32[2,1024]{1,0:T(2,128)S(1)} copy-done((f32[2,1024]{1,0:T(2,128)S(1)}, f32[2,1024]{1,0:T(2,128)}, u32[]{:S(2)}) %copy-start.4) | copy-done | bytes 8216
  20.3 4.7 %tables.1 = (bf16[64,128]{1,0:T(8,128)(2,1)S(1)}, bf16[512,256]{1,0:T(8,128)(2,1)S(1)}, bf16[512,256]{1,0:T(8,128)(2,1)S(1)}, bf16[64,512]{1,0:T(8,128)(2,1)S(1)}, bf16[64,512]{1,0:T(8,128)(2,1)S(1)}) custom-call(f32[2,8,1024]{2,1,0:T(8,128)S(1)} %copy-done.2, bf16[2,1024,1024]{2,1,0:T(8,128)(2,1)S(1)} %copy-done, f32[2,1024]{1,0:T(2,128)S(1)} %copy-done.4, ...), custom_call_target="tpu_custom_call" | custom-call | flops 335544320 | bytes 5242880 | tf_op jit(solution)/shard_map/tables/pallas_call | solution.py:337
  25.0 0.0 all-to-all-done
  25.0 0.9 %stencil.1 = (f32[16,16,256]{2,1,0:T(8,128)S(1)}, f32[16,256]{1,0:T(8,128)S(1)}) custom-call(f32[256,128]{1,0:T(8,128)S(1)} %bitcast.1, bf16[64,128]{1,0:T(8,128)(2,1)S(1)} %get-tuple-element.9.table_ref, bf16[512,256]{1,0:T(8,128)(2,1)S(1)} %get-tuple-element.10.row_high_ref, bf16[512,256]{1,0:T(8,128)(2,1)S(1)} %get-tuple-element.11.row_low_ref), custom_call_target="tpu_custom_call" | custom-call | tf_op jit(solution)/shard_map/stencil/pallas_call | solution.py:351
  26.0 21.3 %all_to_all.10.got_ref = f32[16,16,256]{2,1,0:T(8,128)S(1)} all-to-all(f32[16,16,256]{2,1,0:T(8,128)S(1)} %get-tuple-element.12), channel_id=1, replica_groups=mesh['row'=32,'col'=16] {'col'}, dimensions={0} | all-to-all | bytes 524288 | tf_op jit(solution)/shard_map/all_to_all | solution.py:357
  47.3 1.0 %pattern.1 = (f32[2,4,8,8]{3,2,1,0:T(8,128)}, f32[2,4,32,32]{3,2,1,0:T(8,128)}) custom-call(f32[16,16,256]{2,1,0:T(8,128)S(1)} %all_to_all.10.got_ref, f32[16,256]{1,0:T(8,128)S(1)} %get-tuple-element.13.own_ref, bf16[64,512]{1,0:T(8,128)(2,1)S(1)} %get-tuple-element.14.col_high_ref, bf16[64,512]{1,0:T(8,128)(2,1)S(1)} %get-tuple-element.15.col_low_ref), custom_call_target="tpu_custom_call" | custom-call | tf_op jit(solution)/shard_map/pattern/pallas_call | solution.py:358
Async XLA Ops:
  0.6 0.8 %copy-start.3 = (f32[2,4,8,8]{3,2,1,0:T(8,128)S(1)}, f32[2,4,8,8]{3,2,1,0:T(8,128)}, u32[]{:S(2)}) copy-start(f32[2,4,8,8]{3,2,1,0:T(8,128)} %drive_ref.1) | copy-start | bytes 6148
  1.4 0.7 %copy-start.5 = (s32[8,8]{1,0:T(8,128)S(1)}, s32[8,8]{1,0:T(8,128)}, u32[]{:S(2)}) copy-start(s32[8,8]{1,0:T(8,128)} %flag_ref.1) | copy-start | bytes 772
  2.1 0.7 %copy-start.6 = (s32[8,8]{1,0:T(8,128)S(1)}, s32[8,8]{1,0:T(8,128)}, u32[]{:S(2)}) copy-start(s32[8,8]{1,0:T(8,128)} %port_ref.1) | copy-start | bytes 772
  3.5 21.5 %all-to-all-start = ((f32[32,8,128]{2,1,0:T(8,128)}), f32[32,8,128]{2,1,0:T(8,128)S(1)}, u32[]{:S(2)}, u32[]{:S(2)}) async-start(f32[32,8,128]{2,1,0:T(8,128)} %pack.1), calls=%async_computation | async-start | bytes 262144 | tf_op jit(solution)/shard_map/all_to_all | solution.py:336
  15.5 2.2 %copy-start = (bf16[2,1024,1024]{2,1,0:T(8,128)(2,1)S(1)}, bf16[2,1024,1024]{2,1,0:T(8,128)(2,1)}, u32[]{:S(2)}) copy-start(bf16[2,1024,1024]{2,1,0:T(8,128)(2,1)} %map_ref.1) | copy-start | bytes 12582916
  17.6 1.2 %copy-start.1 = (f32[416,432]{1,0:T(8,128)S(1)}, f32[416,432]{1,0:T(8,128)}, u32[]{:S(2)}) copy-start(f32[416,432]{1,0:T(8,128)} %constant.2.clone.mix_ref) | copy-start | bytes 2156548
  18.8 0.8 %copy-start.2 = (f32[2,8,1024]{2,1,0:T(8,128)S(1)}, f32[2,8,1024]{2,1,0:T(8,128)}, u32[]{:S(2)}) copy-start(f32[2,8,1024]{2,1,0:T(8,128)} %feed_ref.1) | copy-start | bytes 196612
  19.6 0.7 %copy-start.4 = (f32[2,1024]{1,0:T(2,128)S(1)}, f32[2,1024]{1,0:T(2,128)}, u32[]{:S(2)}) copy-start(f32[2,1024]{1,0:T(2,128)} %probe_ref.1) | copy-start | bytes 24580

commit v2 on v1

--- a/solution.py
+++ b/solution.py
@@ -69,6 +69,11 @@
     return high, (value - high.astype(jnp.float32)).astype(jnp.bfloat16)
 
 
+def thirds(value):
+    high, low = halves(value)
+    return high, low, (value - high.astype(jnp.float32) - low.astype(jnp.float32)).astype(jnp.bfloat16)
+
+
 def cosine(turns, length):
     centred = jnp.where(turns >= length // 2, length - turns, turns)
     angle = (length // 4 - centred).astype(jnp.float32) * (2.0 * math.pi / length)
@@ -86,13 +91,24 @@
     return lax.dot_general(left, right, (dims, ((), ())), preferred_element_type=jnp.float32)
 
 
-def dot3(left, right):
+def dot3(left, right, dims=((1,), (0,))):
     high, low = left
     high_right, low_right = right
-    return dot(high, high_right) + (dot(low, high_right) + dot(high, low_right))
-
-
-def pack_kernel(drive_ref, flag_ref, port_ref, out_ref):
+    return dot(high, high_right, dims) + (dot(low, high_right, dims) + dot(high, low_right, dims))
+
+
+def fetch(sems, *pairs, wait=False):
+    copies = [pltpu.make_async_copy(src, dst, sems.at[i]) for i, (src, dst) in enumerate(pairs)]
+    for copy in copies:
+        copy.start()
+    if wait:
+        for copy in copies:
+            copy.wait()
+    return copies
+
+
+def pack_kernel(drive_hbm, flag_hbm, port_hbm, out_ref, drive_ref, flag_ref, port_ref, sems):
+    fetch(sems, (drive_hbm, drive_ref), (flag_hbm, flag_ref), (port_hbm, port_ref), wait=True)
     active = flag_ref[...].astype(jnp.float32)
     pieces = [drive_ref[x, s] * active for x in range(2) for s in range(STATES)]
     pieces.append(port_ref[...].astype(jnp.float32))
@@ -101,9 +117,53 @@
     out_ref[...] = jnp.broadcast_to(packed[None], out_ref.shape)
 
 
-def table_kernel(place, rows, cols, feed_ref, map_ref, probe_ref, mix_ref, table_ref, row_high_ref, row_low_ref, col_high_ref, col_low_ref, hops_ref):
+def twiddles(place, rows, cols, row_high_ref, row_low_ref, col_high_ref, col_low_ref):
     row_at, col_at = place()
+    span = OVER * rows
+    r = lax.broadcasted_iota(jnp.int32, (rows, LANES), 0)
+    k = lax.broadcasted_iota(jnp.int32, (rows, LANES), 1)
+    samples = OVER * BLOCK
+    turns = (r * (row_at * samples + k)) & (span - 1)
+    cos = jnp.where(k < samples, cosine(turns, span), 0.0)
+    sin = jnp.where(k < samples, cosine((turns - span // 4) & (span - 1), span), 0.0)
+    pick = (k >= samples) & (k < samples + BLOCK) & (r == row_at * BLOCK + k - samples)
+    pick = jnp.where(pick, 1.0, 0.0)
+    turn = jnp.concatenate(
+        [
+            jnp.concatenate([cos + pick, -sin], axis=1),
+            jnp.concatenate([sin, cos + pick], axis=1),
+        ],
+        axis=0,
+    )
+    row_high_ref[...], row_low_ref[...] = halves(turn)
+
+    span = OVER * cols
+    shape = (samples, 2 * cols)
+    q = lax.broadcasted_iota(jnp.int32, shape, 0) + col_at * samples
+    k = lax.broadcasted_iota(jnp.int32, shape, 1)
+    c = (k // 16) * BLOCK + k % 16 - REACH
+    inside = (k % 16 < WIDE) & (c >= 0) & (c < cols)
+    turns = (q * c) & (span - 1)
+    scale = (rows * cols) ** -0.5
+    cos = jnp.where(inside, cosine(turns, span) * scale, 0.0)
+    sin = jnp.where(inside, cosine((turns - span // 4) & (span - 1), span) * scale, 0.0)
+    turn = jnp.concatenate(
+        [jnp.concatenate([cos, sin], axis=1), jnp.concatenate([-sin, cos], axis=1)], axis=0
+    )
+    col_high_ref[...], col_low_ref[...] = halves(turn)
+
+
+def table_kernel(
+    place, rows, cols, feed_hbm, map_hbm, probe_hbm, mix_hbm,
+    table_ref, row_high_ref, row_low_ref, col_high_ref, col_low_ref,
+    feed_ref, map_ref, probe_ref, mix_ref, hops_ref, sems,
+):
     edge = feed_ref.shape[2] // 4
+    chunks = [(map_hbm.at[:, pl.ds(a * edge, edge)], map_ref.at[:, pl.ds(a * edge, edge)]) for a in range(4)]
+    copies = fetch(sems, (feed_hbm, feed_ref), (probe_hbm, probe_ref), *chunks, (mix_hbm, mix_ref))
+    twiddles(place, rows, cols, row_high_ref, row_low_ref, col_high_ref, col_low_ref)
+    copies[0].wait()
+    copies[1].wait()
     units = 4 * edge
 
     def block(value, e):
@@ -120,6 +180,7 @@
             [block(feed_re, e), block(feed_im, e), block(back_re, a), block(back_im, a)], axis=0
         )
         enter = jnp.concatenate(halves(enter), axis=0)
+        copies[2 + a].wait()
         by_re = dot(enter, map_ref[0, a * edge : (a + 1) * edge, :])
         by_im = dot(enter, map_ref[1, a * edge : (a + 1) * edge, :])
         by_re = by_re[0:32] + by_re[32:64]
@@ -155,51 +216,14 @@
         ],
         axis=0,
     )
-    products = lax.dot_general(
-        leave, hops_ref[...], (((1,), (1,)), ((), ())),
-        precision=lax.Precision.HIGHEST, preferred_element_type=jnp.float32,
-    )
+    products = dot3(halves(leave), halves(hops_ref[...]), ((1,), (1,)))
+    copies[6].wait()
     flat = jnp.concatenate([products[:, 8 * k : 8 * k + 8] for k in range(18)], axis=0)
-    table = lax.dot_general(
-        mix_ref[...], flat, (((1,), (0,)), ((), ())),
-        precision=lax.Precision.HIGHEST, preferred_element_type=jnp.float32,
-    )
+    table = dot(mix_ref[...], jnp.concatenate(thirds(flat), axis=1))
+    table = table[:, 0:8] + table[:, 8:16] + table[:, 16:24]
     wide = [table[k * ROWS : (k + 1) * ROWS, :] for k in range(CLASSES)]
     wide.append(jnp.zeros((ROWS, LANES - 8 * CLASSES), jnp.float32))
     table_ref[...] = jnp.concatenate(halves(jnp.concatenate(wide, axis=1)), axis=0)
-
-    span = OVER * rows
-    r = lax.broadcasted_iota(jnp.int32, (rows, LANES), 0)
-    k = lax.broadcasted_iota(jnp.int32, (rows, LANES), 1)
-    samples = OVER * BLOCK
-    turns = (r * (row_at * samples + k)) & (span - 1)
-    cos = jnp.where(k < samples, cosine(turns, span), 0.0)
-    sin = jnp.where(k < samples, cosine((turns - span // 4) & (span - 1), span), 0.0)
-    pick = (k >= samples) & (k < samples + BLOCK) & (r == row_at * BLOCK + k - samples)
-    pick = jnp.where(pick, 1.0, 0.0)
-    turn = jnp.concatenate(
-        [
-            jnp.concatenate([cos + pick, -sin], axis=1),
-            jnp.concatenate([sin, cos + pick], axis=1),
-        ],
-        axis=0,
-    )
-    row_high_ref[...], row_low_ref[...] = halves(turn)
-
-    span = OVER * cols
-    shape = (samples, 2 * cols)
-    q = lax.broadcasted_iota(jnp.int32, shape, 0) + col_at * samples
-    k = lax.broadcasted_iota(jnp.int32, shape, 1)
-    c = (k // 16) * BLOCK + k % 16 - REACH
-    inside = (k % 16 < WIDE) & (c >= 0) & (c < cols)
-    turns = (q * c) & (span - 1)
-    scale = (rows * cols) ** -0.5
-    cos = jnp.where(inside, cosine(turns, span) * scale, 0.0)
-    sin = jnp.where(inside, cosine((turns - span // 4) & (span - 1), span) * scale, 0.0)
-    turn = jnp.concatenate(
-        [jnp.concatenate([cos, sin], axis=1), jnp.concatenate([-sin, cos], axis=1)], axis=0
-    )
-    col_high_ref[...], col_low_ref[...] = halves(turn)
 
 
 def stencil_kernel(place, rows, cols, cells_ref, table_ref, row_high_ref, row_low_ref, out_ref, own_ref, coef_ref):
@@ -314,12 +338,15 @@
     return lax.axis_index("row"), lax.axis_index("col")
 
 
-def call(kernel, out_shape, scratch=(), flops=0, size=0, **options):
+HBM = pl.BlockSpec(memory_space=pltpu.HBM)
+
+
+def call(kernel, out_shape, scratch=(), flops=0, size=0, grant=40960, **options):
     return pl.pallas_call(
         kernel,
         out_shape=out_shape,
         scratch_shapes=list(scratch),
-        compiler_params=pltpu.CompilerParams(vmem_limit_bytes=40 * 1024 * 1024),
+        compiler_params=pltpu.CompilerParams(vmem_limit_bytes=grant * 1024),
         cost_estimate=pl.CostEstimate(flops=flops, bytes_accessed=size, transcendentals=0),
         **options,
     )
@@ -330,10 +357,17 @@
     samples = OVER * BLOCK
     f32, b16 = jnp.float32, jnp.bfloat16
     shape = jax.ShapeDtypeStruct
-    packed = call(pack_kernel, shape((row_blocks, BLOCK, LANES), f32), name="pack")(
-        drive_weights, active_flags, port_index
-    )
+    taken = (drive_weights, active_flags, port_index)
+    packed = call(
+        pack_kernel,
+        shape((row_blocks, BLOCK, LANES), f32),
+        scratch=[pltpu.VMEM(x.shape, x.dtype) for x in taken] + [pltpu.SemaphoreType.DMA((3,))],
+        in_specs=[HBM] * 3,
+        name="pack",
+        grant=61440,
+    )(*taken)
     cells = lax.all_to_all(packed, "row", 0, 0).reshape(rows, LANES)
+    taken = (feed_table, cell_map, probe_weights, jnp.asarray(path_matrix(), b16))
     table, row_high, row_low, col_high, col_low = call(
         functools.partial(table_kernel, place, rows, cols),
         (
@@ -343,11 +377,14 @@
             shape((2 * samples, 4 * cols), b16),
             shape((2 * samples, 4 * cols), b16),
         ),
-        scratch=[pltpu.VMEM((144, cell_map.shape[1]), f32)],
+        scratch=[pltpu.VMEM(x.shape, x.dtype) for x in taken]
+        + [pltpu.VMEM((144, cell_map.shape[1]), f32), pltpu.SemaphoreType.DMA((7,))],
+        in_specs=[HBM] * 4,
         flops=2 * 80 * 2 * 1024 * 1024,
         size=5 * 1024 * 1024,
         name="tables",
-    )(feed_table, cell_map, probe_weights, jnp.asarray(path_matrix()))
+        grant=54272,
+    )(*taken)
     pieces, own = call(
         functools.partial(stencil_kernel, place, rows, cols),
         (shape((col_blocks, 16, 2 * LANES), f32), shape((16, 2 * LANES), f32)),

time: 48.8 us -> 46.6 us (0.955)
  local copies, waits for them, and re-layouts: 7 us -> 1.53 us
  waiting for transfers between devices: 0.01 us -> 2.22 us
  Pallas kernels: 7.37 us -> 8.39 us
    unnamed x14 -> x4, local copies, waits for them, and re-layouts: 7 us -> 1.53 us
    all_to_all x1, waiting for transfers between devices: 0.01 us -> 2.22 us  [body(): cells = lax.all_to_all(packed, 'row', 0, 0).reshape(rows, LANES)]
    pallas_call x1, Pallas kernels: 0.74 us -> 1.53 us  [body(): call(pack_kernel, shape((row_blocks, BLOCK, LANES), f32), scratch=[pltpu....]
  transfers between devices with their start and end apart: 1 -> 1, of which waited for: 0 -> 1; matrix products, arithmetic and copies ran while one was open for 0% -> 0% of each run, Pallas kernels for 10% -> 11%
where the time goes in v2:
time: 46.6 us; the launch traced here: 46.3 us
  blocking collectives  21.5 us (46%)
  starting transfers between devices  11.9 us (26%)
  Pallas kernels  8.39 us (18%)
  waiting for transfers between devices  2.22 us (5%)
  local copies, waits for them, and re-layouts  1.53 us (3%)
  between operations  0.67 us (1%)
    all_to_all x1, blocking collectives, body(): got = lax.all_to_all(pieces, 'col', 0, 0)  21.5 us
    all_to_all x1, starting transfers between devices, body(): cells = lax.all_to_all(packed, 'row', 0, 0).reshape(rows, LANES)  11.9 us
    pallas_call x1, Pallas kernels, body(): call(functools.partial(table_kernel, place, rows, cols), (shape((2 * ROWS...  4.93 us
    all_to_all x1, waiting for transfers between devices, body(): cells = lax.all_to_all(packed, 'row', 0, 0).reshape(rows, LANES)  2.22 us
    unnamed x4, local copies, waits for them, and re-layouts  1.53 us
    pallas_call x1, Pallas kernels, body(): call(pack_kernel, shape((row_blocks, BLOCK, LANES), f32), scratch=[pltpu....  1.53 us
    pallas_call x1, Pallas kernels, body(): call(functools.partial(pattern_kernel, place, col_blocks), (shape((2, STA...  1.03 us
  transfers between devices with their start and end apart: 1, of which 1 were waited for; matrix products, arithmetic and copies ran while one was open for 0% of the time, Pallas kernels for 11%

profile of v2, /device:TPU:8, one launch (start us, length us, event | category | flops | bytes accessed | tf_op | source)
XLA Modules:
  0.0 46.3 jit_solution(13183067903965282950)
XLA Ops:
  0.6 1.5 %pack.1 = f32[32,8,128]{2,1,0:T(8,128)} custom-call(f32[2,4,8,8]{3,2,1,0:T(8,128)} %drive_hbm.1, s32[8,8]{1,0:T(8,128)} %flag_hbm.1, s32[8,8]{1,0:T(8,128)} %port_hbm.1), custom_call_target="tpu_custom_call" | custom-call | tf_op jit(solution)/shard_map/pack/pallas_call | solution.py:361
  2.2 11.9 %all-to-all-start = ((f32[32,8,128]{2,1,0:T(8,128)}), f32[32,8,128]{2,1,0:T(8,128)S(1)}, u32[]{:S(2)}, u32[]{:S(2)}) async-start(f32[32,8,128]{2,1,0:T(8,128)} %pack.1), calls=%async_computation | async-start | bytes 262144 | tf_op jit(solution)/shard_map/all_to_all | solution.py:369
  14.1 0.0 copy-start
  14.1 0.8 %copy-done = f32[2,8,1024]{2,1,0:T(8,128)S(1)} copy-done((f32[2,8,1024]{2,1,0:T(8,128)S(1)}, f32[2,8,1024]{2,1,0:T(8,128)}, u32[]{:S(2)}) %copy-start) | copy-done | bytes 65560
  15.0 0.0 copy-start.1
  15.0 0.7 %copy-done.1 = f32[2,1024]{1,0:T(2,128)S(1)} copy-done((f32[2,1024]{1,0:T(2,128)S(1)}, f32[2,1024]{1,0:T(2,128)}, u32[]{:S(2)}) %copy-start.1) | copy-done | bytes 8216
  15.7 4.9 %tables.1 = (bf16[64,128]{1,0:T(8,128)(2,1)S(1)}, bf16[512,256]{1,0:T(8,128)(2,1)S(1)}, bf16[512,256]{1,0:T(8,128)(2,1)S(1)}, bf16[64,512]{1,0:T(8,128)(2,1)S(1)}, bf16[64,512]{1,0:T(8,128)(2,1)S(1)}) custom-call(f32[2,8,1024]{2,1,0:T(8,128)S(1)} %copy-done, bf16[2,1024,1024]{2,1,0:T(8,128)(2,1)} %map_hbm.1, f32[2,1024]{1,0:T(2,128)S(1)} %copy-done.1, ...), custom_call_target="tpu_custom_call" | custom-call | flops 335544320 | bytes 5242880 | tf_op jit(solution)/shard_map/tables/pallas_call | solution.py:371
  20.6 2.2 %all-to-all-done = f32[32,8,128]{2,1,0:T(8,128)S(1)} async-done(((f32[32,8,128]{2,1,0:T(8,128)}), f32[32,8,128]{2,1,0:T(8,128)S(1)}, u32[]{:S(2)}, u32[]{:S(2)}) %all-to-all-start) | async-done | bytes 131104 | tf_op jit(solution)/shard_map/all_to_all | solution.py:369
  22.8 0.9 %stencil.1 = (f32[16,16,256]{2,1,0:T(8,128)S(1)}, f32[16,256]{1,0:T(8,128)S(1)}) custom-call(f32[256,128]{1,0:T(8,128)S(1)} %bitcast.1, bf16[64,128]{1,0:T(8,128)(2,1)S(1)} %get-tuple-element.9.table_ref, bf16[512,256]{1,0:T(8,128)(2,1)S(1)} %get-tuple-element.10.row_high_ref, bf16[512,256]{1,0:T(8,128)(2,1)S(1)} %get-tuple-element.11.row_low_ref), custom_call_target="tpu_custom_call" | custom-call | tf_op jit(solution)/shard_map/stencil/pallas_call | solution.py:388
  23.7 21.5 %all_to_all.10.got_ref = f32[16,16,256]{2,1,0:T(8,128)S(1)} all-to-all(f32[16,16,256]{2,1,0:T(8,128)S(1)} %get-tuple-element.12), channel_id=1, replica_groups=mesh['row'=32,'col'=16] {'col'}, dimensions={0} | all-to-all | bytes 524288 | tf_op jit(solution)/shard_map/all_to_all | solution.py:394
  45.2 1.0 %pattern.1 = (f32[2,4,8,8]{3,2,1,0:T(8,128)}, f32[2,4,32,32]{3,2,1,0:T(8,128)}) custom-call(f32[16,16,256]{2,1,0:T(8,128)S(1)} %all_to_all.10.got_ref, f32[16,256]{1,0:T(8,128)S(1)} %get-tuple-element.13.own_ref, bf16[64,512]{1,0:T(8,128)(2,1)S(1)} %get-tuple-element.14.col_high_ref, bf16[64,512]{1,0:T(8,128)(2,1)S(1)} %get-tuple-element.15.col_low_ref), custom_call_target="tpu_custom_call" | custom-call | tf_op jit(solution)/shard_map/pattern/pallas_call | solution.py:395
Async XLA Ops:
  2.2 20.7 %all-to-all-start = ((f32[32,8,128]{2,1,0:T(8,128)}), f32[32,8,128]{2,1,0:T(8,128)S(1)}, u32[]{:S(2)}, u32[]{:S(2)}) async-start(f32[32,8,128]{2,1,0:T(8,128)} %pack.1), calls=%async_computation | async-start | bytes 262144 | tf_op jit(solution)/shard_map/all_to_all | solution.py:369
  14.1 0.8 %copy-start = (f32[2,8,1024]{2,1,0:T(8,128)S(1)}, f32[2,8,1024]{2,1,0:T(8,128)}, u32[]{:S(2)}) copy-start(f32[2,8,1024]{2,1,0:T(8,128)} %feed_hbm.1) | copy-start | bytes 196612
  15.0 0.7 %copy-start.1 = (f32[2,1024]{1,0:T(2,128)S(1)}, f32[2,1024]{1,0:T(2,128)}, u32[]{:S(2)}) copy-start(f32[2,1024]{1,0:T(2,128)} %probe_hbm.1) | copy-start | bytes 24580

commit v3 on v2

--- a/solution.py
+++ b/solution.py
@@ -16,6 +16,7 @@
 REACH = 2
 WIDE = 12
 LANES = 128
+USED = 72
 
 relaxation = 0.75
 reflect_re = -0.3
@@ -26,6 +27,7 @@
     (dr, dc) for dr in range(-2, 3) for dc in range(-2, 3) if abs(dr) + abs(dc) <= 2
 )
 CLASSES = 13
+SHARE = 52
 ROWS = 32
 
 
@@ -107,17 +109,7 @@
     return copies
 
 
-def pack_kernel(drive_hbm, flag_hbm, port_hbm, out_ref, drive_ref, flag_ref, port_ref, sems):
-    fetch(sems, (drive_hbm, drive_ref), (flag_hbm, flag_ref), (port_hbm, port_ref), wait=True)
-    active = flag_ref[...].astype(jnp.float32)
-    pieces = [drive_ref[x, s] * active for x in range(2) for s in range(STATES)]
-    pieces.append(port_ref[...].astype(jnp.float32))
-    pieces.append(jnp.zeros((BLOCK, LANES - 9 * BLOCK), jnp.float32))
-    packed = jnp.concatenate(pieces, axis=1)
-    out_ref[...] = jnp.broadcast_to(packed[None], out_ref.shape)
-
-
-def twiddles(place, rows, cols, row_high_ref, row_low_ref, col_high_ref, col_low_ref):
+def turn_kernel(place, rows, cols, row_high_ref, row_low_ref, col_high_ref, col_low_ref):
     row_at, col_at = place()
     span = OVER * rows
     r = lax.broadcasted_iota(jnp.int32, (rows, LANES), 0)
@@ -153,15 +145,10 @@
     col_high_ref[...], col_low_ref[...] = halves(turn)
 
 
-def table_kernel(
-    place, rows, cols, feed_hbm, map_hbm, probe_hbm, mix_hbm,
-    table_ref, row_high_ref, row_low_ref, col_high_ref, col_low_ref,
-    feed_ref, map_ref, probe_ref, mix_ref, hops_ref, sems,
-):
+def make_table(feed_hbm, map_hbm, probe_hbm, mix_hbm, table_ref, feed_ref, map_ref, probe_ref, mix_ref, hops_ref, sems):
     edge = feed_ref.shape[2] // 4
     chunks = [(map_hbm.at[:, pl.ds(a * edge, edge)], map_ref.at[:, pl.ds(a * edge, edge)]) for a in range(4)]
     copies = fetch(sems, (feed_hbm, feed_ref), (probe_hbm, probe_ref), *chunks, (mix_hbm, mix_ref))
-    twiddles(place, rows, cols, row_high_ref, row_low_ref, col_high_ref, col_low_ref)
     copies[0].wait()
     copies[1].wait()
     units = 4 * edge
@@ -223,10 +210,40 @@
     table = table[:, 0:8] + table[:, 8:16] + table[:, 16:24]
     wide = [table[k * ROWS : (k + 1) * ROWS, :] for k in range(CLASSES)]
     wide.append(jnp.zeros((ROWS, LANES - 8 * CLASSES), jnp.float32))
-    table_ref[...] = jnp.concatenate(halves(jnp.concatenate(wide, axis=1)), axis=0)
-
-
-def stencil_kernel(place, rows, cols, cells_ref, table_ref, row_high_ref, row_low_ref, out_ref, own_ref, coef_ref):
+    table_ref[...] = jnp.concatenate(wide, axis=1)
+
+
+def maker(row_at):
+    return row_at % 16 < 4, row_at % 4 + 4 * (row_at // 16)
+
+
+def pack_kernel(
+    place, drive_hbm, flag_hbm, port_hbm, feed_hbm, map_hbm, probe_hbm, mix_hbm, out_ref,
+    drive_ref, flag_ref, port_ref, feed_ref, map_ref, probe_ref, mix_ref, hops_ref, table_ref, piece_ref, sems, table_sems,
+):
+    makes, share = maker(place()[0])
+    fetch(sems, (drive_hbm, drive_ref), (flag_hbm, flag_ref), (port_hbm, port_ref), wait=True)
+    active = flag_ref[...].astype(jnp.float32)
+    pieces = [drive_ref[x, s] * active for x in range(2) for s in range(STATES)]
+    pieces.append(port_ref[...].astype(jnp.float32))
+    pieces.append(jnp.zeros((BLOCK, LANES - USED), jnp.float32))
+    piece_ref[...] = jnp.concatenate(pieces, axis=1)
+
+    @pl.when(makes)
+    def _():
+        make_table(
+            feed_hbm, map_hbm, probe_hbm, mix_hbm, table_ref,
+            feed_ref, map_ref, probe_ref, mix_ref, hops_ref, table_sems,
+        )
+        part = table_ref[pl.ds(pl.multiple_of(share // 2 * 8, 8), 8), :]
+        part = jnp.where(share % 2 == 0, pltpu.roll(part, USED, axis=1), pltpu.roll(part, USED - SHARE, axis=1))
+        lane = lax.broadcasted_iota(jnp.int32, (BLOCK, LANES), 1)
+        piece_ref[...] += jnp.where((lane >= USED) & (lane < USED + SHARE), part, 0.0)
+
+    out_ref[...] = jnp.broadcast_to(piece_ref[...][None], out_ref.shape)
+
+
+def stencil_kernel(place, rows, cols, cells_ref, row_high_ref, row_low_ref, out_ref, own_ref, coef_ref):
     _, col_at = place()
     across = cells_ref[...].T
     amps = [[across[(x * 4 + s) * 8 : (x * 4 + s) * 8 + 8] for s in range(STATES)] for x in range(2)]
@@ -239,7 +256,14 @@
         return jnp.where(mask, 1.0, 0.0)
 
     north, south, north2, south2 = flag(r == 0), flag(r == rows - 1), flag(r == 1), flag(r == rows - 2)
-    table = table_ref[...]
+    lane = lax.broadcasted_iota(jnp.int32, (BLOCK, LANES), 1)
+    parts = [cells_ref[(k % 4 + 16 * (k // 4)) * BLOCK : (k % 4 + 16 * (k // 4) + 1) * BLOCK, :] for k in range(8)]
+    firsts = [jnp.where(lane < SHARE, pltpu.roll(part, LANES - USED, axis=1), 0.0) for part in parts[0::2]]
+    seconds = [
+        jnp.where((lane >= SHARE) & (lane < 2 * SHARE), pltpu.roll(part, LANES - USED + SHARE, axis=1), 0.0)
+        for part in parts[1::2]
+    ]
+    table = jnp.concatenate(halves(jnp.concatenate([a + b for a, b in zip(firsts, seconds)], axis=0)), axis=0)
     for j in range(BLOCK):
         c = col_at * BLOCK + j
         west, east = flag(c == 0), flag(c == cols - 1)
@@ -357,40 +381,44 @@
     samples = OVER * BLOCK
     f32, b16 = jnp.float32, jnp.bfloat16
     shape = jax.ShapeDtypeStruct
-    taken = (drive_weights, active_flags, port_index)
+    taken = (
+        drive_weights, active_flags, port_index,
+        feed_table, cell_map, probe_weights, jnp.asarray(path_matrix(), b16),
+    )
     packed = call(
-        pack_kernel,
+        functools.partial(pack_kernel, place),
         shape((row_blocks, BLOCK, LANES), f32),
-        scratch=[pltpu.VMEM(x.shape, x.dtype) for x in taken] + [pltpu.SemaphoreType.DMA((3,))],
-        in_specs=[HBM] * 3,
+        scratch=[pltpu.VMEM(x.shape, x.dtype) for x in taken]
+        + [
+            pltpu.VMEM((144, cell_map.shape[1]), f32),
+            pltpu.VMEM((ROWS, LANES), f32),
+            pltpu.VMEM((BLOCK, LANES), f32),
+            pltpu.SemaphoreType.DMA((3,)),
+            pltpu.SemaphoreType.DMA((7,)),
+        ],
+        in_specs=[HBM] * 7,
         name="pack",
         grant=61440,
     )(*taken)
     cells = lax.all_to_all(packed, "row", 0, 0).reshape(rows, LANES)
-    taken = (feed_table, cell_map, probe_weights, jnp.asarray(path_matrix(), b16))
-    table, row_high, row_low, col_high, col_low = call(
-        functools.partial(table_kernel, place, rows, cols),
+    row_high, row_low, col_high, col_low = call(
+        functools.partial(turn_kernel, place, rows, cols),
         (
-            shape((2 * ROWS, LANES), b16),
             shape((2 * rows, 2 * LANES), b16),
             shape((2 * rows, 2 * LANES), b16),
             shape((2 * samples, 4 * cols), b16),
             shape((2 * samples, 4 * cols), b16),
         ),
-        scratch=[pltpu.VMEM(x.shape, x.dtype) for x in taken]
-        + [pltpu.VMEM((144, cell_map.shape[1]), f32), pltpu.SemaphoreType.DMA((7,))],
-        in_specs=[HBM] * 4,
         flops=2 * 80 * 2 * 1024 * 1024,
         size=5 * 1024 * 1024,
-        name="tables",
-        grant=54272,
-    )(*taken)
+        name="turns",
+    )()
     pieces, own = call(
         functools.partial(stencil_kernel, place, rows, cols),
         (shape((col_blocks, 16, 2 * LANES), f32), shape((16, 2 * LANES), f32)),
         scratch=[pltpu.VMEM((rows // LANES, BLOCK * ROWS, LANES), f32)],
         name="stencil",
-    )(cells, table, row_high, row_low)
+    )(cells, row_high, row_low)
     got = lax.all_to_all(pieces, "col", 0, 0)
     return call(
         functools.partial(pattern_kernel, place, col_blocks),

time: 46.6 us -> 46.6 us (level)
  waiting for transfers between devices: 2.22 us -> 8.32 us
  starting transfers between devices: 11.9 us -> 9.44 us
  blocking collectives: 21.5 us -> 19.1 us
  local copies, waits for them, and re-layouts: 1.53 us -> 0 us
  Pallas kernels: 8.39 us -> 8.86 us
    all_to_all x1, waiting for transfers between devices: 2.22 us -> 8.32 us  [body(): cells = lax.all_to_all(packed, 'row', 0, 0).reshape(rows, LANES)]
    all_to_all x1, starting transfers between devices: 11.9 us -> 9.44 us  [body(): cells = lax.all_to_all(packed, 'row', 0, 0).reshape(rows, LANES)]
    all_to_all x1, blocking collectives: 21.5 us -> 19.1 us  [body(): got = lax.all_to_all(pieces, 'col', 0, 0)]
    unnamed x4 -> x0, local copies, waits for them, and re-layouts: 1.53 us -> none
  transfers between devices with their start and end apart: 1 -> 1, of which waited for: 1 -> 1; matrix products, arithmetic and copies ran while one was open for 0% -> 0% of each run, Pallas kernels for 11% -> 1%
where the time goes in v3:
time: 46.6 us; the launch traced here: 46.4 us
  blocking collectives  19.1 us (41%)
  starting transfers between devices  9.44 us (20%)
  Pallas kernels  8.86 us (19%)
  waiting for transfers between devices  8.32 us (18%)
  between operations  0.66 us (1%)
    all_to_all x1, blocking collectives, body(): got = lax.all_to_all(pieces, 'col', 0, 0)  19.1 us
    all_to_all x1, starting transfers between devices, body(): cells = lax.all_to_all(packed, 'row', 0, 0).reshape(rows, LANES)  9.44 us
    all_to_all x1, waiting for transfers between devices, body(): cells = lax.all_to_all(packed, 'row', 0, 0).reshape(rows, LANES)  8.32 us
    pallas_call x1, Pallas kernels, body(): call(functools.partial(pack_kernel, place), shape((row_blocks, BLOCK, LAN...  6.53 us
    pallas_call x1, Pallas kernels, body(): call(functools.partial(pattern_kernel, place, col_blocks), (shape((2, STA...  1.03 us
  transfers between devices with their start and end apart: 1, of which 1 were waited for; matrix products, arithmetic and copies ran while one was open for 0% of the time, Pallas kernels for 1%

profile of v3, /device:TPU:8, one launch (start us, length us, event | category | flops | bytes accessed | tf_op | source)
XLA Modules:
  0.0 46.4 jit_solution(16597990268902902633)
XLA Ops:
  0.6 6.5 %pack.1 = f32[32,8,128]{2,1,0:T(8,128)} custom-call(f32[2,4,8,8]{3,2,1,0:T(8,128)} %drive_hbm.1, s32[8,8]{1,0:T(8,128)} %flag_hbm.1, s32[8,8]{1,0:T(8,128)} %port_hbm.1, f32[2,8,1024]{2,1,0:T(8,128)} %feed_hbm.1, bf16[2,1024,1024]{2,1,0:T(8,128)(2,1)} %map_hbm.1, f32[2,1024]{1,0:T(2,128)} %probe_hbm.1, bf16[416,432]{1,0:T(8,128)(2,1)} %constant.2.clone.mix_hbm), custom_call_target="tpu_custom_call" | custom-call | tf_op jit(solution)/shard_map/pack/pallas_call | solution.py:388
  7.2 9.4 %all-to-all-start = ((f32[32,8,128]{2,1,0:T(8,128)}), f32[32,8,128]{2,1,0:T(8,128)S(1)}, u32[]{:S(2)}, u32[]{:S(2)}) async-start(f32[32,8,128]{2,1,0:T(8,128)} %pack.1), calls=%async_computation | async-start | bytes 262144 | tf_op jit(solution)/shard_map/all_to_all | solution.py:403
  16.6 0.4 turns.1
  17.0 8.3 %all-to-all-done = f32[32,8,128]{2,1,0:T(8,128)S(1)} async-done(((f32[32,8,128]{2,1,0:T(8,128)}), f32[32,8,128]{2,1,0:T(8,128)S(1)}, u32[]{:S(2)}, u32[]{:S(2)}) %all-to-all-start) | async-done | bytes 131104 | tf_op jit(solution)/shard_map/all_to_all | solution.py:403
  25.3 0.9 %stencil.1 = (f32[16,16,256]{2,1,0:T(8,128)S(1)}, f32[16,256]{1,0:T(8,128)S(1)}) custom-call(f32[256,128]{1,0:T(8,128)S(1)} %bitcast.1, bf16[512,256]{1,0:T(8,128)(2,1)S(1)} %get-tuple-element.8.row_high_ref, bf16[512,256]{1,0:T(8,128)(2,1)S(1)} %get-tuple-element.9.row_low_ref), custom_call_target="tpu_custom_call" | custom-call | tf_op jit(solution)/shard_map/stencil/pallas_call | solution.py:416
  26.3 19.1 %all_to_all.10.got_ref = f32[16,16,256]{2,1,0:T(8,128)S(1)} all-to-all(f32[16,16,256]{2,1,0:T(8,128)S(1)} %get-tuple-element.10), channel_id=1, replica_groups=mesh['row'=32,'col'=16] {'col'}, dimensions={0} | all-to-all | bytes 524288 | tf_op jit(solution)/shard_map/all_to_all | solution.py:422
  45.3 1.0 %pattern.1 = (f32[2,4,8,8]{3,2,1,0:T(8,128)}, f32[2,4,32,32]{3,2,1,0:T(8,128)}) custom-call(f32[16,16,256]{2,1,0:T(8,128)S(1)} %all_to_all.10.got_ref, f32[16,256]{1,0:T(8,128)S(1)} %get-tuple-element.11.own_ref, bf16[64,512]{1,0:T(8,128)(2,1)S(1)} %get-tuple-element.12.col_high_ref, bf16[64,512]{1,0:T(8,128)(2,1)S(1)} %get-tuple-element.13.col_low_ref), custom_call_target="tpu_custom_call" | custom-call | tf_op jit(solution)/shard_map/pattern/pallas_call | solution.py:423
Async XLA Ops:
  7.2 18.2 %all-to-all-start = ((f32[32,8,128]{2,1,0:T(8,128)}), f32[32,8,128]{2,1,0:T(8,128)S(1)}, u32[]{:S(2)}, u32[]{:S(2)}) async-start(f32[32,8,128]{2,1,0:T(8,128)} %pack.1), calls=%async_computation | async-start | bytes 262144 | tf_op jit(solution)/shard_map/all_to_all | solution.py:403

commit v4 on v3

--- a/solution.py
+++ b/solution.py
@@ -16,6 +16,7 @@
 REACH = 2
 WIDE = 12
 LANES = 128
+PIECE = 26
 USED = 72
 
 relaxation = 0.75
@@ -130,18 +131,22 @@
     row_high_ref[...], row_low_ref[...] = halves(turn)
 
     span = OVER * cols
-    shape = (samples, 2 * cols)
+    blocks = cols // BLOCK
+    shape = (samples, blocks * PIECE)
     q = lax.broadcasted_iota(jnp.int32, shape, 0) + col_at * samples
     k = lax.broadcasted_iota(jnp.int32, shape, 1)
-    c = (k // 16) * BLOCK + k % 16 - REACH
-    inside = (k % 16 < WIDE) & (c >= 0) & (c < cols)
+    block = jnp.zeros(shape, jnp.int32)
+    for b in range(1, blocks):
+        block = block + jnp.where(k >= b * PIECE, 1, 0)
+    at = k - block * PIECE
+    imaginary = at >= WIDE
+    c = block * BLOCK + at - jnp.where(imaginary, WIDE, 0) - REACH
+    inside = (at < 2 * WIDE) & (c >= 0) & (c < cols)
     turns = (q * c) & (span - 1)
     scale = (rows * cols) ** -0.5
     cos = jnp.where(inside, cosine(turns, span) * scale, 0.0)
     sin = jnp.where(inside, cosine((turns - span // 4) & (span - 1), span) * scale, 0.0)
-    turn = jnp.concatenate(
-        [jnp.concatenate([cos, sin], axis=1), jnp.concatenate([-sin, cos], axis=1)], axis=0
-    )
+    turn = jnp.concatenate([jnp.where(imaginary, sin, cos), jnp.where(imaginary, cos, -sin)], axis=0)
     col_high_ref[...], col_low_ref[...] = halves(turn)
 
 
@@ -315,6 +320,7 @@
     lane = lax.broadcasted_iota(jnp.int32, (8, LANES), 1)
     first, second = lane < samples, (lane >= samples) & (lane < samples + BLOCK)
     nothing = jnp.zeros((16, LANES), jnp.float32)
+    mains, nears = [], []
     for x in range(2):
         main, near = nothing, nothing
         for i, dc in enumerate(range(-2, 3)):
@@ -329,33 +335,46 @@
             shift = REACH + dc
             main = main + (pltpu.roll(for_main, shift, axis=0) if shift else for_main)
             near = near + (pltpu.roll(for_near, shift, axis=0) if shift else for_near)
-        piece = jnp.concatenate([main[0:12], near[0:2], near[10:12]], axis=0)
-        out_ref[:, :, x * LANES : (x + 1) * LANES] = jnp.broadcast_to(piece[None], (out_ref.shape[0], 16, LANES))
+        mains.append(main[0:WIDE])
+        nears.append(
+            near[0:1] + pltpu.roll(near, BLOCK, axis=1)[1:2]
+            + pltpu.roll(near, 2 * BLOCK, axis=1)[10:11] + pltpu.roll(near, 3 * BLOCK, axis=1)[11:12]
+        )
         own_ref[:, x * LANES : (x + 1) * LANES] = near
+    piece = jnp.concatenate(mains + nears, axis=0)
+    four = jnp.concatenate([piece] * 4, axis=0)
+    for i in range(out_ref.shape[0] // (4 * PIECE)):
+        out_ref[i * 4 * PIECE : (i + 1) * 4 * PIECE, :] = four
 
 
 def pattern_kernel(place, blocks, got_ref, own_ref, col_high_ref, col_low_ref, currents_ref, far_ref):
     _, col_at = place()
     samples = OVER * BLOCK
-    got = jnp.concatenate(
-        [got_ref[:, :, x * LANES : (x + 1) * LANES].reshape(blocks * 16, LANES) for x in range(2)], axis=0
-    )
-    far = dot3((col_high_ref[...], col_low_ref[...]), halves(got))
+    far = dot3((col_high_ref[...], col_low_ref[...]), halves(got_ref[...]))
     far = jnp.concatenate([far, jnp.zeros_like(far)], axis=0).T
     for x in range(2):
         for s in range(STATES):
             far_ref[x, s] = far[s * samples : (s + 1) * samples, x * samples : (x + 1) * samples]
     left, right = jnp.maximum(col_at - 1, 0), jnp.minimum(col_at + 1, blocks - 1)
-    from_left = jnp.where(col_at > 0, 1.0, 0.0) * got_ref[left]
-    from_right = jnp.where(col_at < blocks - 1, 1.0, 0.0) * got_ref[right]
+    has_left, has_right = jnp.where(col_at > 0, 1.0, 0.0), jnp.where(col_at < blocks - 1, 1.0, 0.0)
     own = own_ref[...]
-    whole = jnp.concatenate(
-        [own[2:4] + from_left[14:16], own[4:8], own[8:10] + from_right[12:14]], axis=0
-    )
     for x in range(2):
-        flat = jnp.concatenate([whole[:, x * LANES : (x + 1) * LANES], jnp.zeros((LANES - 8, LANES), jnp.float32)], axis=0).T
+        from_left = has_left * got_ref[pl.ds(left * PIECE + 2 * WIDE + x, 1), :]
+        from_right = has_right * got_ref[pl.ds(right * PIECE + 2 * WIDE + x, 1), :]
+        mine = own[:, x * LANES : (x + 1) * LANES]
+        whole = jnp.concatenate(
+            [
+                mine[2:3] + pltpu.roll(from_left, LANES - 2 * BLOCK, axis=1),
+                mine[3:4] + pltpu.roll(from_left, LANES - 3 * BLOCK, axis=1),
+                mine[4:8],
+                mine[8:9] + from_right,
+                mine[9:10] + pltpu.roll(from_right, LANES - BLOCK, axis=1),
+                jnp.zeros((LANES - BLOCK, LANES), jnp.float32),
+            ],
+            axis=0,
+        ).T
         for s in range(STATES):
-            currents_ref[x, s] = flat[s * samples : s * samples + BLOCK, 0:BLOCK]
+            currents_ref[x, s] = whole[s * samples : s * samples + BLOCK, 0:BLOCK]
 
 
 def spot():
@@ -406,8 +425,8 @@
         (
             shape((2 * rows, 2 * LANES), b16),
             shape((2 * rows, 2 * LANES), b16),
-            shape((2 * samples, 4 * cols), b16),
-            shape((2 * samples, 4 * cols), b16),
+            shape((2 * samples, col_blocks * PIECE), b16),
+            shape((2 * samples, col_blocks * PIECE), b16),
         ),
         flops=2 * 80 * 2 * 1024 * 1024,
         size=5 * 1024 * 1024,
@@ -415,16 +434,16 @@
     )()
     pieces, own = call(
         functools.partial(stencil_kernel, place, rows, cols),
-        (shape((col_blocks, 16, 2 * LANES), f32), shape((16, 2 * LANES), f32)),
+        (shape((col_blocks * PIECE, LANES), f32), shape((16, 2 * LANES), f32)),
         scratch=[pltpu.VMEM((rows // LANES, BLOCK * ROWS, LANES), f32)],
         name="stencil",
     )(cells, row_high, row_low)
-    got = lax.all_to_all(pieces, "col", 0, 0)
+    got = lax.all_to_all(pieces.reshape(col_blocks, PIECE // 2, 2, LANES), "col", 0, 0)
     return call(
         functools.partial(pattern_kernel, place, col_blocks),
         (shape((2, STATES, BLOCK, BLOCK), f32), shape((2, STATES, samples, samples), f32)),
         name="pattern",
-    )(got, own, col_high, col_low)
+    )(got.reshape(col_blocks * PIECE, LANES), own, col_high, col_low)
 
 
 def solution(mesh):

time: 46.6 us -> 45.7 us (0.981)
  blocking collectives: 19.1 us -> 18.1 us
    all_to_all x1, blocking collectives: 19.1 us -> 18.1 us  [body(): lax.all_to_all(pieces.reshape(col_blocks, PIECE // 2, 2, LANES), 'col', 0...]
where the time goes in v4:
time: 45.7 us; the launch traced here: 45.4 us
  blocking collectives  18.1 us (40%)
  starting transfers between devices  9.44 us (21%)
  Pallas kernels  8.98 us (20%)
  waiting for transfers between devices  8.25 us (18%)
  between operations  0.66 us (1%)
    all_to_all x1, blocking collectives, body(): lax.all_to_all(pieces.reshape(col_blocks, PIECE // 2, 2, LANES), 'col', 0...  18.1 us
    all_to_all x1, starting transfers between devices, body(): cells = lax.all_to_all(packed, 'row', 0, 0).reshape(rows, LANES)  9.44 us
    all_to_all x1, waiting for transfers between devices, body(): cells = lax.all_to_all(packed, 'row', 0, 0).reshape(rows, LANES)  8.25 us
    pallas_call x1, Pallas kernels, body(): call(functools.partial(pack_kernel, place), shape((row_blocks, BLOCK, LAN...  6.53 us
    pallas_call x1, Pallas kernels, body(): call(functools.partial(pattern_kernel, place, col_blocks), (shape((2, STA...  1.04 us
    pallas_call x1, Pallas kernels, body(): call(functools.partial(stencil_kernel, place, rows, cols), (shape((col_bl...  0.96 us
  transfers between devices with their start and end apart: 1, of which 1 were waited for; matrix products, arithmetic and copies ran while one was open for 0% of the time, Pallas kernels for 1%

profile of v4, /device:TPU:8, one launch (start us, length us, event | category | flops | bytes accessed | tf_op | source)
XLA Modules:
  0.0 45.4 jit_solution(143996376390628153)
XLA Ops:
  0.6 6.5 %pack.1 = f32[32,8,128]{2,1,0:T(8,128)} custom-call(f32[2,4,8,8]{3,2,1,0:T(8,128)} %drive_hbm.1, s32[8,8]{1,0:T(8,128)} %flag_hbm.1, s32[8,8]{1,0:T(8,128)} %port_hbm.1, f32[2,8,1024]{2,1,0:T(8,128)} %feed_hbm.1, bf16[2,1024,1024]{2,1,0:T(8,128)(2,1)} %map_hbm.1, f32[2,1024]{1,0:T(2,128)} %probe_hbm.1, bf16[416,432]{1,0:T(8,128)(2,1)} %constant.2.clone.mix_hbm), custom_call_target="tpu_custom_call" | custom-call | tf_op jit(solution)/shard_map/pack/pallas_call | solution.py:407
  7.2 9.4 %all-to-all-start = ((f32[32,8,128]{2,1,0:T(8,128)}), f32[32,8,128]{2,1,0:T(8,128)S(1)}, u32[]{:S(2)}, u32[]{:S(2)}) async-start(f32[32,8,128]{2,1,0:T(8,128)} %pack.1), calls=%async_computation | async-start | bytes 262144 | tf_op jit(solution)/shard_map/all_to_all | solution.py:422
  16.6 0.4 turns.1
  17.1 8.3 %all-to-all-done = f32[32,8,128]{2,1,0:T(8,128)S(1)} async-done(((f32[32,8,128]{2,1,0:T(8,128)}), f32[32,8,128]{2,1,0:T(8,128)S(1)}, u32[]{:S(2)}, u32[]{:S(2)}) %all-to-all-start) | async-done | bytes 131104 | tf_op jit(solution)/shard_map/all_to_all | solution.py:422
  25.3 1.0 %stencil.1 = (f32[416,128]{1,0:T(8,128)S(1)}, f32[16,256]{1,0:T(8,128)S(1)}) custom-call(f32[256,128]{1,0:T(8,128)S(1)} %bitcast.4, bf16[512,256]{1,0:T(8,128)(2,1)S(1)} %get-tuple-element.8.row_high_ref, bf16[512,256]{1,0:T(8,128)(2,1)S(1)} %get-tuple-element.9.row_low_ref), custom_call_target="tpu_custom_call" | custom-call | tf_op jit(solution)/shard_map/stencil/pallas_call | solution.py:435
  26.3 18.1 %all_to_all.10 = f32[16,13,2,128]{3,2,1,0:T(2,128)S(1)} all-to-all(f32[16,13,2,128]{3,2,1,0:T(2,128)S(1)} %bitcast.5), channel_id=1, replica_groups=mesh['row'=32,'col'=16] {'col'}, dimensions={0} | all-to-all | bytes 425984 | tf_op jit(solution)/shard_map/all_to_all | solution.py:441
  44.4 1.0 %pattern.1 = (f32[2,4,8,8]{3,2,1,0:T(8,128)}, f32[2,4,32,32]{3,2,1,0:T(8,128)}) custom-call(f32[416,128]{1,0:T(8,128)S(1)} %bitcast.3, f32[16,256]{1,0:T(8,128)S(1)} %get-tuple-element.11.own_ref, bf16[64,416]{1,0:T(8,128)(2,1)S(1)} %get-tuple-element.12.col_high_ref, bf16[64,416]{1,0:T(8,128)(2,1)S(1)} %get-tuple-element.13.col_low_ref), custom_call_target="tpu_custom_call" | custom-call | tf_op jit(solution)/shard_map/pattern/pallas_call | solution.py:442
Async XLA Ops:
  7.2 18.2 %all-to-all-start = ((f32[32,8,128]{2,1,0:T(8,128)}), f32[32,8,128]{2,1,0:T(8,128)S(1)}, u32[]{:S(2)}, u32[]{:S(2)}) async-start(f32[32,8,128]{2,1,0:T(8,128)} %pack.1), calls=%async_computation | async-start | bytes 262144 | tf_op jit(solution)/shard_map/all_to_all | solution.py:422

commit v5 on v4

--- a/solution.py
+++ b/solution.py
@@ -16,6 +16,8 @@
 REACH = 2
 WIDE = 12
 LANES = 128
+FIRST_ROW = 10
+FIRST_COL = 10
 PIECE = 26
 USED = 72
 
@@ -140,7 +142,7 @@
         block = block + jnp.where(k >= b * PIECE, 1, 0)
     at = k - block * PIECE
     imaginary = at >= WIDE
-    c = block * BLOCK + at - jnp.where(imaginary, WIDE, 0) - REACH
+    c = (block + FIRST_COL) % blocks * BLOCK + at - jnp.where(imaginary, WIDE, 0) - REACH
     inside = (at < 2 * WIDE) & (c >= 0) & (c < cols)
     turns = (q * c) & (span - 1)
     scale = (rows * cols) ** -0.5
@@ -250,7 +252,8 @@
 
 def stencil_kernel(place, rows, cols, cells_ref, row_high_ref, row_low_ref, out_ref, own_ref, coef_ref):
     _, col_at = place()
-    across = cells_ref[...].T
+    start = (rows // BLOCK - FIRST_ROW) * BLOCK
+    across = jnp.concatenate([cells_ref[start:, :], cells_ref[:start, :]], axis=0).T
     amps = [[across[(x * 4 + s) * 8 : (x * 4 + s) * 8 + 8] for s in range(STATES)] for x in range(2)]
     ports = across[64:72]
 
@@ -262,7 +265,8 @@
 
     north, south, north2, south2 = flag(r == 0), flag(r == rows - 1), flag(r == 1), flag(r == rows - 2)
     lane = lax.broadcasted_iota(jnp.int32, (BLOCK, LANES), 1)
-    parts = [cells_ref[(k % 4 + 16 * (k // 4)) * BLOCK : (k % 4 + 16 * (k // 4) + 1) * BLOCK, :] for k in range(8)]
+    makers = [(k % 4 + 16 * (k // 4) - FIRST_ROW) * BLOCK % rows for k in range(8)]
+    parts = [cells_ref[k : k + BLOCK, :] for k in makers]
     firsts = [jnp.where(lane < SHARE, pltpu.roll(part, LANES - USED, axis=1), 0.0) for part in parts[0::2]]
     seconds = [
         jnp.where((lane >= SHARE) & (lane < 2 * SHARE), pltpu.roll(part, LANES - USED + SHARE, axis=1), 0.0)
@@ -355,7 +359,7 @@
     for x in range(2):
         for s in range(STATES):
             far_ref[x, s] = far[s * samples : (s + 1) * samples, x * samples : (x + 1) * samples]
-    left, right = jnp.maximum(col_at - 1, 0), jnp.minimum(col_at + 1, blocks - 1)
+    left, right = (col_at + blocks - 1 - FIRST_COL) % blocks, (col_at + blocks + 1 - FIRST_COL) % blocks
     has_left, has_right = jnp.where(col_at > 0, 1.0, 0.0), jnp.where(col_at < blocks - 1, 1.0, 0.0)
     own = own_ref[...]
     for x in range(2):
@@ -395,6 +399,12 @@
     )
 
 
+def exchange(pieces, axis, first):
+    size = pieces.shape[0]
+    order = [(first + k) % size for k in range(size)]
+    return lax.all_to_all(pieces, axis, 0, 0, axis_index_groups=[order])
+
+
 def body(row_blocks, col_blocks, place, active_flags, port_index, drive_weights, feed_table, cell_map, probe_weights):
     rows, cols = row_blocks * BLOCK, col_blocks * BLOCK
     samples = OVER * BLOCK
@@ -419,7 +429,7 @@
         name="pack",
         grant=61440,
     )(*taken)
-    cells = lax.all_to_all(packed, "row", 0, 0).reshape(rows, LANES)
+    cells = exchange(packed, "row", FIRST_ROW).reshape(rows, LANES)
     row_high, row_low, col_high, col_low = call(
         functools.partial(turn_kernel, place, rows, cols),
         (
@@ -438,7 +448,7 @@
         scratch=[pltpu.VMEM((rows // LANES, BLOCK * ROWS, LANES), f32)],
         name="stencil",
     )(cells, row_high, row_low)
-    got = lax.all_to_all(pieces.reshape(col_blocks, PIECE // 2, 2, LANES), "col", 0, 0)
+    got = exchange(pieces.reshape(col_blocks, PIECE // 2, 2, LANES), "col", FIRST_COL)
     return call(
         functools.partial(pattern_kernel, place, col_blocks),
         (shape((2, STATES, BLOCK, BLOCK), f32), shape((2, STATES, samples, samples), f32)),

time: 45.7 us -> 41.7 us (0.912)
  the two profiles are of different devices: /device:TPU:8 before, /device:TPU:1 now
where the time goes in v5:
time: 41.7 us; the launch traced here: 41.4 us
  blocking collectives  14.1 us (34%)
  starting transfers between devices  13 us (31%)
  Pallas kernels  8.98 us (22%)
  waiting for transfers between devices  4.61 us (11%)
  between operations  0.66 us (2%)
    all_to_all x1, blocking collectives, exchange(): return lax.all_to_all(pieces, axis, 0, 0, axis_index_groups=[order])  14.1 us
    all_to_all x1, starting transfers between devices, exchange(): return lax.all_to_all(pieces, axis, 0, 0, axis_index_groups=[order])  13 us
    pallas_call x1, Pallas kernels, body(): call(functools.partial(pack_kernel, place), shape((row_blocks, BLOCK, LAN...  6.53 us
    all_to_all x1, waiting for transfers between devices, exchange(): return lax.all_to_all(pieces, axis, 0, 0, axis_index_groups=[order])  4.61 us
    pallas_call x1, Pallas kernels, body(): call(functools.partial(pattern_kernel, place, col_blocks), (shape((2, STA...  1.04 us
    pallas_call x1, Pallas kernels, body(): call(functools.partial(stencil_kernel, place, rows, cols), (shape((col_bl...  0.96 us
  transfers between devices with their start and end apart: 1, of which 1 were waited for; matrix products, arithmetic and copies ran while one was open for 0% of the time, Pallas kernels for 1%

profile of v5, /device:TPU:1, one launch (start us, length us, event | category | flops | bytes accessed | tf_op | source)
XLA Modules:
  0.0 41.4 jit_solution(3315305683721915567)
XLA Ops:
  0.6 6.5 %pack.1 = f32[32,8,128]{2,1,0:T(8,128)} custom-call(f32[2,4,8,8]{3,2,1,0:T(8,128)} %drive_hbm.1, s32[8,8]{1,0:T(8,128)} %flag_hbm.1, s32[8,8]{1,0:T(8,128)} %port_hbm.1, f32[2,8,1024]{2,1,0:T(8,128)} %feed_hbm.1, bf16[2,1024,1024]{2,1,0:T(8,128)(2,1)} %map_hbm.1, f32[2,1024]{1,0:T(2,128)} %probe_hbm.1, bf16[416,432]{1,0:T(8,128)(2,1)} %constant.2.clone.mix_hbm), custom_call_target="tpu_custom_call" | custom-call | tf_op jit(solution)/shard_map/pack/pallas_call | solution.py:417
  7.2 13.0 %all-to-all-start = ((f32[32,8,128]{2,1,0:T(8,128)}), f32[32,8,128]{2,1,0:T(8,128)S(1)}, u32[]{:S(2)}, u32[]{:S(2)}) async-start(f32[32,8,128]{2,1,0:T(8,128)} %pack.1), calls=%async_computation | async-start | bytes 262144 | tf_op jit(solution)/shard_map/all_to_all | solution.py:405
  20.2 0.4 %turns.1 = (bf16[512,256]{1,0:T(8,128)(2,1)S(1)}, bf16[512,256]{1,0:T(8,128)(2,1)S(1)}, bf16[64,416]{1,0:T(8,128)(2,1)S(1)}, bf16[64,416]{1,0:T(8,128)(2,1)S(1)}) custom-call(), custom_call_target="tpu_custom_call" | custom-call | flops 335544320 | bytes 5242880 | tf_op jit(solution)/shard_map/turns/pallas_call | solution.py:433
  20.7 4.6 %all-to-all-done = f32[32,8,128]{2,1,0:T(8,128)S(1)} async-done(((f32[32,8,128]{2,1,0:T(8,128)}), f32[32,8,128]{2,1,0:T(8,128)S(1)}, u32[]{:S(2)}, u32[]{:S(2)}) %all-to-all-start) | async-done | bytes 131104 | tf_op jit(solution)/shard_map/all_to_all | solution.py:405
  25.3 1.0 %stencil.1 = (f32[416,128]{1,0:T(8,128)S(1)}, f32[16,256]{1,0:T(8,128)S(1)}) custom-call(f32[256,128]{1,0:T(8,128)S(1)} %bitcast.4, bf16[512,256]{1,0:T(8,128)(2,1)S(1)} %get-tuple-element.8.row_high_ref, bf16[512,256]{1,0:T(8,128)(2,1)S(1)} %get-tuple-element.9.row_low_ref), custom_call_target="tpu_custom_call" | custom-call | tf_op jit(solution)/shard_map/stencil/pallas_call | solution.py:445
  26.2 14.1 %all_to_all.10 = f32[16,13,2,128]{3,2,1,0:T(2,128)S(1)} all-to-all(f32[16,13,2,128]{3,2,1,0:T(2,128)S(1)} %bitcast.5), channel_id=1, replica_groups={{10,11,12,13,14,15,0,1,2,3,4,5,6,7,8,9},{26,27,28,29,30,31,16,17,18,19,..., dimensions={0} | all-to-all | bytes 425984 | tf_op jit(solution)/shard_map/all_to_all | solution.py:405
  40.4 1.0 %pattern.1 = (f32[2,4,8,8]{3,2,1,0:T(8,128)}, f32[2,4,32,32]{3,2,1,0:T(8,128)}) custom-call(f32[416,128]{1,0:T(8,128)S(1)} %bitcast.3, f32[16,256]{1,0:T(8,128)S(1)} %get-tuple-element.11.own_ref, bf16[64,416]{1,0:T(8,128)(2,1)S(1)} %get-tuple-element.12.col_high_ref, bf16[64,416]{1,0:T(8,128)(2,1)S(1)} %get-tuple-element.13.col_low_ref), custom_call_target="tpu_custom_call" | custom-call | tf_op jit(solution)/shard_map/pattern/pallas_call | solution.py:452
Async XLA Ops:
  7.2 18.1 %all-to-all-start = ((f32[32,8,128]{2,1,0:T(8,128)}), f32[32,8,128]{2,1,0:T(8,128)S(1)}, u32[]{:S(2)}, u32[]{:S(2)}) async-start(f32[32,8,128]{2,1,0:T(8,128)} %pack.1), calls=%async_computation | async-start | bytes 262144 | tf_op jit(solution)/shard_map/all_to_all | solution.py:405

commit v6 on v4

--- a/solution.py
+++ b/solution.py
@@ -16,6 +16,8 @@
 REACH = 2
 WIDE = 12
 LANES = 128
+ROW_ORDER = tuple((15 + k) % 32 for k in range(32))
+COL_ORDER = tuple((14 + k) % 16 for k in range(16))
 PIECE = 26
 USED = 72
 
@@ -97,7 +99,9 @@
 def dot3(left, right, dims=((1,), (0,))):
     high, low = left
     high_right, low_right = right
-    return dot(high, high_right, dims) + (dot(low, high_right, dims) + dot(high, low_right, dims))
+    both = dot(jnp.concatenate([high, low], axis=0), high_right, dims)
+    size = high.shape[0]
+    return both[:size] + (both[size:] + dot(high, low_right, dims))
 
 
 def fetch(sems, *pairs, wait=False):
@@ -135,10 +139,11 @@
     shape = (samples, blocks * PIECE)
     q = lax.broadcasted_iota(jnp.int32, shape, 0) + col_at * samples
     k = lax.broadcasted_iota(jnp.int32, shape, 1)
-    block = jnp.zeros(shape, jnp.int32)
+    block = jnp.full(shape, COL_ORDER[0], jnp.int32)
+    at = k
     for b in range(1, blocks):
-        block = block + jnp.where(k >= b * PIECE, 1, 0)
-    at = k - block * PIECE
+        block = block + jnp.where(k >= b * PIECE, COL_ORDER[b] - COL_ORDER[b - 1], 0)
+        at = at - jnp.where(k >= b * PIECE, PIECE, 0)
     imaginary = at >= WIDE
     c = block * BLOCK + at - jnp.where(imaginary, WIDE, 0) - REACH
     inside = (at < 2 * WIDE) & (c >= 0) & (c < cols)
@@ -250,7 +255,8 @@
 
 def stencil_kernel(place, rows, cols, cells_ref, row_high_ref, row_low_ref, out_ref, own_ref, coef_ref):
     _, col_at = place()
-    across = cells_ref[...].T
+    slots = [ROW_ORDER.index(k) * BLOCK for k in range(rows // BLOCK)]
+    across = jnp.concatenate([cells_ref[k : k + BLOCK, :] for k in slots], axis=0).T
     amps = [[across[(x * 4 + s) * 8 : (x * 4 + s) * 8 + 8] for s in range(STATES)] for x in range(2)]
     ports = across[64:72]
 
@@ -262,7 +268,8 @@
 
     north, south, north2, south2 = flag(r == 0), flag(r == rows - 1), flag(r == 1), flag(r == rows - 2)
     lane = lax.broadcasted_iota(jnp.int32, (BLOCK, LANES), 1)
-    parts = [cells_ref[(k % 4 + 16 * (k // 4)) * BLOCK : (k % 4 + 16 * (k // 4) + 1) * BLOCK, :] for k in range(8)]
+    makers = [slots[k % 4 + 16 * (k // 4)] for k in range(8)]
+    parts = [cells_ref[k : k + BLOCK, :] for k in makers]
     firsts = [jnp.where(lane < SHARE, pltpu.roll(part, LANES - USED, axis=1), 0.0) for part in parts[0::2]]
     seconds = [
         jnp.where((lane >= SHARE) & (lane < 2 * SHARE), pltpu.roll(part, LANES - USED + SHARE, axis=1), 0.0)
@@ -355,7 +362,10 @@
     for x in range(2):
         for s in range(STATES):
             far_ref[x, s] = far[s * samples : (s + 1) * samples, x * samples : (x + 1) * samples]
-    left, right = jnp.maximum(col_at - 1, 0), jnp.minimum(col_at + 1, blocks - 1)
+    left, right = 0, 0
+    for b in range(blocks):
+        left = jnp.where(col_at == b + 1, COL_ORDER.index(b), left)
+        right = jnp.where(col_at == b - 1, COL_ORDER.index(b), right)
     has_left, has_right = jnp.where(col_at > 0, 1.0, 0.0), jnp.where(col_at < blocks - 1, 1.0, 0.0)
     own = own_ref[...]
     for x in range(2):
@@ -395,6 +405,10 @@
     )
 
 
+def exchange(pieces, axis, order):
+    return lax.all_to_all(pieces, axis, 0, 0, axis_index_groups=[list(order)])
+
+
 def body(row_blocks, col_blocks, place, active_flags, port_index, drive_weights, feed_table, cell_map, probe_weights):
     rows, cols = row_blocks * BLOCK, col_blocks * BLOCK
     samples = OVER * BLOCK
@@ -419,7 +433,7 @@
         name="pack",
         grant=61440,
     )(*taken)
-    cells = lax.all_to_all(packed, "row", 0, 0).reshape(rows, LANES)
+    cells = exchange(packed, "row", ROW_ORDER).reshape(rows, LANES)
     row_high, row_low, col_high, col_low = call(
         functools.partial(turn_kernel, place, rows, cols),
         (
@@ -438,7 +452,7 @@
         scratch=[pltpu.VMEM((rows // LANES, BLOCK * ROWS, LANES), f32)],
         name="stencil",
     )(cells, row_high, row_low)
-    got = lax.all_to_all(pieces.reshape(col_blocks, PIECE // 2, 2, LANES), "col", 0, 0)
+    got = exchange(pieces.reshape(col_blocks, PIECE // 2, 2, LANES), "col", COL_ORDER)
     return call(
         functools.partial(pattern_kernel, place, col_blocks),
         (shape((2, STATES, BLOCK, BLOCK), f32), shape((2, STATES, samples, samples), f32)),

time: 45.7 us -> 40.1 us (0.88)
  blocking collectives: 18.1 us -> 14.3 us
  waiting for transfers between devices: 8.25 us -> 6.56 us
    all_to_all x1, blocking collectives: 18.1 us -> 14.3 us  [exchange(): return lax.all_to_all(pieces, axis, 0, 0, axis_index_groups=[list(order)])]
    all_to_all x1, waiting for transfers between devices: 8.25 us -> 6.56 us  [exchange(): return lax.all_to_all(pieces, axis, 0, 0, axis_index_groups=[list(order)])]
where the time goes in v6:
time: 40.1 us; the launch traced here: 39.8 us
  blocking collectives  14.3 us (36%)
  starting transfers between devices  9.65 us (24%)
  Pallas kernels  8.58 us (21%)
  waiting for transfers between devices  6.56 us (16%)
  between operations  0.66 us (2%)
    all_to_all x1, blocking collectives, exchange(): return lax.all_to_all(pieces, axis, 0, 0, axis_index_groups=[list(order)])  14.3 us
    all_to_all x1, starting transfers between devices, exchange(): return lax.all_to_all(pieces, axis, 0, 0, axis_index_groups=[list(order)])  9.65 us
    all_to_all x1, waiting for transfers between devices, exchange(): return lax.all_to_all(pieces, axis, 0, 0, axis_index_groups=[list(order)])  6.56 us
    pallas_call x1, Pallas kernels, body(): call(functools.partial(pack_kernel, place), shape((row_blocks, BLOCK, LAN...  6.16 us
    pallas_call x1, Pallas kernels, body(): call(functools.partial(pattern_kernel, place, col_blocks), (shape((2, STA...  1.02 us
    pallas_call x1, Pallas kernels, body(): call(functools.partial(stencil_kernel, place, rows, cols), (shape((col_bl...  0.96 us
  transfers between devices with their start and end apart: 1, of which 1 were waited for; matrix products, arithmetic and copies ran while one was open for 0% of the time, Pallas kernels for 1%

profile of v6, /device:TPU:8, one launch (start us, length us, event | category | flops | bytes accessed | tf_op | source)
XLA Modules:
  0.0 39.8 jit_solution(15623122670496883359)
XLA Ops:
  0.6 6.2 %pack.1 = f32[32,8,128]{2,1,0:T(8,128)} custom-call(f32[2,4,8,8]{3,2,1,0:T(8,128)} %drive_hbm.1, s32[8,8]{1,0:T(8,128)} %flag_hbm.1, s32[8,8]{1,0:T(8,128)} %port_hbm.1, f32[2,8,1024]{2,1,0:T(8,128)} %feed_hbm.1, bf16[2,1024,1024]{2,1,0:T(8,128)(2,1)} %map_hbm.1, f32[2,1024]{1,0:T(2,128)} %probe_hbm.1, bf16[416,432]{1,0:T(8,128)(2,1)} %constant.2.clone.mix_hbm), custom_call_target="tpu_custom_call" | custom-call | tf_op jit(solution)/shard_map/pack/pallas_call | solution.py:421
  6.8 9.7 %all-to-all-start = ((f32[32,8,128]{2,1,0:T(8,128)}), f32[32,8,128]{2,1,0:T(8,128)S(1)}, u32[]{:S(2)}, u32[]{:S(2)}) async-start(f32[32,8,128]{2,1,0:T(8,128)} %pack.1), calls=%async_computation | async-start | bytes 262144 | tf_op jit(solution)/shard_map/all_to_all | solution.py:409
  16.5 0.4 %turns.1 = (bf16[512,256]{1,0:T(8,128)(2,1)S(1)}, bf16[512,256]{1,0:T(8,128)(2,1)S(1)}, bf16[64,416]{1,0:T(8,128)(2,1)S(1)}, bf16[64,416]{1,0:T(8,128)(2,1)S(1)}) custom-call(), custom_call_target="tpu_custom_call" | custom-call | flops 335544320 | bytes 5242880 | tf_op jit(solution)/shard_map/turns/pallas_call | solution.py:437
  16.9 6.6 %all-to-all-done = f32[32,8,128]{2,1,0:T(8,128)S(1)} async-done(((f32[32,8,128]{2,1,0:T(8,128)}), f32[32,8,128]{2,1,0:T(8,128)S(1)}, u32[]{:S(2)}, u32[]{:S(2)}) %all-to-all-start) | async-done | bytes 131104 | tf_op jit(solution)/shard_map/all_to_all | solution.py:409
  23.5 1.0 %stencil.1 = (f32[416,128]{1,0:T(8,128)S(1)}, f32[16,256]{1,0:T(8,128)S(1)}) custom-call(f32[256,128]{1,0:T(8,128)S(1)} %bitcast.4, bf16[512,256]{1,0:T(8,128)(2,1)S(1)} %get-tuple-element.8.row_high_ref, bf16[512,256]{1,0:T(8,128)(2,1)S(1)} %get-tuple-element.9.row_low_ref), custom_call_target="tpu_custom_call" | custom-call | tf_op jit(solution)/shard_map/stencil/pallas_call | solution.py:449
  24.4 14.3 %all_to_all.10 = f32[16,13,2,128]{3,2,1,0:T(2,128)S(1)} all-to-all(f32[16,13,2,128]{3,2,1,0:T(2,128)S(1)} %bitcast.5), channel_id=1, replica_groups={{14,15,0,1,2,3,4,5,6,7,8,9,10,11,12,13},{30,31,16,17,18,19,20,21,22,23,..., dimensions={0} | all-to-all | bytes 425984 | tf_op jit(solution)/shard_map/all_to_all | solution.py:409
  38.8 1.0 %pattern.1 = (f32[2,4,8,8]{3,2,1,0:T(8,128)}, f32[2,4,32,32]{3,2,1,0:T(8,128)}) custom-call(f32[416,128]{1,0:T(8,128)S(1)} %bitcast.3, f32[16,256]{1,0:T(8,128)S(1)} %get-tuple-element.11.own_ref, bf16[64,416]{1,0:T(8,128)(2,1)S(1)} %get-tuple-element.12.col_high_ref, bf16[64,416]{1,0:T(8,128)(2,1)S(1)} %get-tuple-element.13.col_low_ref), custom_call_target="tpu_custom_call" | custom-call | tf_op jit(solution)/shard_map/pattern/pallas_call | solution.py:456
Async XLA Ops:
  6.8 16.7 %all-to-all-start = ((f32[32,8,128]{2,1,0:T(8,128)}), f32[32,8,128]{2,1,0:T(8,128)S(1)}, u32[]{:S(2)}, u32[]{:S(2)}) async-start(f32[32,8,128]{2,1,0:T(8,128)} %pack.1), calls=%async_computation | async-start | bytes 262144 | tf_op jit(solution)/shard_map/all_to_all | solution.py:409

commit v7 on v6

--- a/solution.py
+++ b/solution.py
@@ -104,17 +104,14 @@
     return both[:size] + (both[size:] + dot(high, low_right, dims))
 
 
-def fetch(sems, *pairs, wait=False):
+def fetch(sems, *pairs):
     copies = [pltpu.make_async_copy(src, dst, sems.at[i]) for i, (src, dst) in enumerate(pairs)]
     for copy in copies:
         copy.start()
-    if wait:
-        for copy in copies:
-            copy.wait()
     return copies
 
 
-def turn_kernel(place, rows, cols, row_high_ref, row_low_ref, col_high_ref, col_low_ref):
+def make_turns(place, rows, cols, row_high_ref, row_low_ref, col_high_ref, col_low_ref):
     row_at, col_at = place()
     span = OVER * rows
     r = lax.broadcasted_iota(jnp.int32, (rows, LANES), 0)
@@ -228,11 +225,15 @@
 
 
 def pack_kernel(
-    place, drive_hbm, flag_hbm, port_hbm, feed_hbm, map_hbm, probe_hbm, mix_hbm, out_ref,
+    place, rows, cols, drive_hbm, flag_hbm, port_hbm, feed_hbm, map_hbm, probe_hbm, mix_hbm,
+    out_ref, row_high_ref, row_low_ref, col_high_ref, col_low_ref,
     drive_ref, flag_ref, port_ref, feed_ref, map_ref, probe_ref, mix_ref, hops_ref, table_ref, piece_ref, sems, table_sems,
 ):
     makes, share = maker(place()[0])
-    fetch(sems, (drive_hbm, drive_ref), (flag_hbm, flag_ref), (port_hbm, port_ref), wait=True)
+    copies = fetch(sems, (drive_hbm, drive_ref), (flag_hbm, flag_ref), (port_hbm, port_ref))
+    make_turns(place, rows, cols, row_high_ref, row_low_ref, col_high_ref, col_low_ref)
+    for copy in copies:
+        copy.wait()
     active = flag_ref[...].astype(jnp.float32)
     pieces = [drive_ref[x, s] * active for x in range(2) for s in range(STATES)]
     pieces.append(port_ref[...].astype(jnp.float32))
@@ -266,6 +267,7 @@
     def flag(mask):
         return jnp.where(mask, 1.0, 0.0)
 
+    none = jnp.zeros((8, rows), jnp.float32)
     north, south, north2, south2 = flag(r == 0), flag(r == rows - 1), flag(r == 1), flag(r == rows - 2)
     lane = lax.broadcasted_iota(jnp.int32, (BLOCK, LANES), 1)
     makers = [slots[k % 4 + 16 * (k // 4)] for k in range(8)]
@@ -278,16 +280,16 @@
     table = jnp.concatenate(halves(jnp.concatenate([a + b for a, b in zip(firsts, seconds)], axis=0)), axis=0)
     for j in range(BLOCK):
         c = col_at * BLOCK + j
-        west, east = flag(c == 0), flag(c == cols - 1)
-        west2, east2 = flag(c == 1), flag(c == cols - 2)
         chosen = flag(jnp.broadcast_to(ports[j : j + 1], (8, rows)) == sub)
         at_north, at_south = chosen * north, chosen * south
-        kinds = [
-            chosen, at_north, at_south, chosen * west, chosen * east,
-            chosen * north2, chosen * south2, chosen * west2, chosen * east2,
-            at_north * west, at_north * east, at_south * west, at_south * east,
-            jnp.zeros((LANES - 8 * CLASSES, rows), jnp.float32),
-        ]
+        kinds = [chosen, at_north, at_south, none, none, chosen * north2, chosen * south2] + [none] * 6
+        if j in (0, BLOCK - 1):
+            edge, first, second = (flag(c == 0), 9, 11) if j == 0 else (flag(c == cols - 1), 10, 12)
+            kinds[3 if j == 0 else 4] = chosen * edge
+            kinds[first], kinds[second] = at_north * edge, at_south * edge
+        if j in (1, BLOCK - 2):
+            kinds[7 if j == 1 else 8] = chosen * (flag(c == 1) if j == 1 else flag(c == cols - 2))
+        kinds.append(jnp.zeros((LANES - 8 * CLASSES, rows), jnp.float32))
         found = dot(table, jnp.concatenate(kinds, axis=0).astype(jnp.bfloat16))
         found = found[0:ROWS] + found[ROWS : 2 * ROWS]
         for half in range(rows // LANES):
@@ -358,33 +360,31 @@
     _, col_at = place()
     samples = OVER * BLOCK
     far = dot3((col_high_ref[...], col_low_ref[...]), halves(got_ref[...]))
-    far = jnp.concatenate([far, jnp.zeros_like(far)], axis=0).T
-    for x in range(2):
-        for s in range(STATES):
-            far_ref[x, s] = far[s * samples : (s + 1) * samples, x * samples : (x + 1) * samples]
     left, right = 0, 0
     for b in range(blocks):
         left = jnp.where(col_at == b + 1, COL_ORDER.index(b), left)
         right = jnp.where(col_at == b - 1, COL_ORDER.index(b), right)
     has_left, has_right = jnp.where(col_at > 0, 1.0, 0.0), jnp.where(col_at < blocks - 1, 1.0, 0.0)
     own = own_ref[...]
+    stacked = [far]
     for x in range(2):
         from_left = has_left * got_ref[pl.ds(left * PIECE + 2 * WIDE + x, 1), :]
         from_right = has_right * got_ref[pl.ds(right * PIECE + 2 * WIDE + x, 1), :]
         mine = own[:, x * LANES : (x + 1) * LANES]
-        whole = jnp.concatenate(
-            [
-                mine[2:3] + pltpu.roll(from_left, LANES - 2 * BLOCK, axis=1),
-                mine[3:4] + pltpu.roll(from_left, LANES - 3 * BLOCK, axis=1),
-                mine[4:8],
-                mine[8:9] + from_right,
-                mine[9:10] + pltpu.roll(from_right, LANES - BLOCK, axis=1),
-                jnp.zeros((LANES - BLOCK, LANES), jnp.float32),
-            ],
-            axis=0,
-        ).T
+        stacked += [
+            mine[2:3] + pltpu.roll(from_left, LANES - 2 * BLOCK, axis=1),
+            mine[3:4] + pltpu.roll(from_left, LANES - 3 * BLOCK, axis=1),
+            mine[4:8],
+            mine[8:9] + from_right,
+            mine[9:10] + pltpu.roll(from_right, LANES - BLOCK, axis=1),
+        ]
+    stacked.append(jnp.zeros((LANES - 2 * samples - 2 * BLOCK, LANES), jnp.float32))
+    flat = jnp.concatenate(stacked, axis=0).T
+    for x in range(2):
+        at = 2 * samples + x * BLOCK
         for s in range(STATES):
-            currents_ref[x, s] = whole[s * samples : s * samples + BLOCK, 0:BLOCK]
+            far_ref[x, s] = flat[s * samples : (s + 1) * samples, x * samples : (x + 1) * samples]
+            currents_ref[x, s] = flat[s * samples : s * samples + BLOCK, at : at + BLOCK]
 
 
 def spot():
@@ -418,9 +418,15 @@
         drive_weights, active_flags, port_index,
         feed_table, cell_map, probe_weights, jnp.asarray(path_matrix(), b16),
     )
-    packed = call(
-        functools.partial(pack_kernel, place),
-        shape((row_blocks, BLOCK, LANES), f32),
+    packed, row_high, row_low, col_high, col_low = call(
+        functools.partial(pack_kernel, place, rows, cols),
+        (
+            pltpu.VMEM((row_blocks, BLOCK, LANES), f32),
+            pltpu.VMEM((2 * rows, 2 * LANES), b16),
+            pltpu.VMEM((2 * rows, 2 * LANES), b16),
+            pltpu.VMEM((2 * samples, col_blocks * PIECE), b16),
+            pltpu.VMEM((2 * samples, col_blocks * PIECE), b16),
+        ),
         scratch=[pltpu.VMEM(x.shape, x.dtype) for x in taken]
         + [
             pltpu.VMEM((144, cell_map.shape[1]), f32),
@@ -431,21 +437,9 @@
         ],
         in_specs=[HBM] * 7,
         name="pack",
-        grant=61440,
+        grant=57344,
     )(*taken)
     cells = exchange(packed, "row", ROW_ORDER).reshape(rows, LANES)
-    row_high, row_low, col_high, col_low = call(
-        functools.partial(turn_kernel, place, rows, cols),
-        (
-            shape((2 * rows, 2 * LANES), b16),
-            shape((2 * rows, 2 * LANES), b16),
-            shape((2 * samples, col_blocks * PIECE), b16),
-            shape((2 * samples, col_blocks * PIECE), b16),
-        ),
-        flops=2 * 80 * 2 * 1024 * 1024,
-        size=5 * 1024 * 1024,
-        name="turns",
-    )()
     pieces, own = call(
         functools.partial(stencil_kernel, place, rows, cols),
         (shape((col_blocks * PIECE, LANES), f32), shape((16, 2 * LANES), f32)),

time: 40.1 us -> 38.7 us (0.965)
  the two profiles are of different devices: /device:TPU:8 before, /device:TPU:14 now
where the time goes in v7:
time: 38.7 us; the launch traced here: 38.5 us
  blocking collectives  30.4 us (79%)
  Pallas kernels  7.46 us (19%)
  between operations  0.65 us (2%)
    all_to_all x2, blocking collectives, exchange(): return lax.all_to_all(pieces, axis, 0, 0, axis_index_groups=[list(order)])  30.4 us
    pallas_call x1, Pallas kernels, body(): call(functools.partial(pack_kernel, place, rows, cols), (pltpu.VMEM((row_...  5.51 us
    pallas_call x1, Pallas kernels, body(): call(functools.partial(pattern_kernel, place, col_blocks), (shape((2, STA...  1.03 us
    pallas_call x1, Pallas kernels, body(): call(functools.partial(stencil_kernel, place, rows, cols), (shape((col_bl...  0.93 us

profile of v7, /device:TPU:14, one launch (start us, length us, event | category | flops | bytes accessed | tf_op | source)
XLA Modules:
  0.0 38.5 jit_solution(6185866576592651051)
XLA Ops:
  0.6 5.5 %pack.1 = (f32[32,8,128]{2,1,0:T(8,128)S(1)}, bf16[512,256]{1,0:T(8,128)(2,1)S(1)}, bf16[512,256]{1,0:T(8,128)(2,1)S(1)}, bf16[64,416]{1,0:T(8,128)(2,1)S(1)}, bf16[64,416]{1,0:T(8,128)(2,1)S(1)}) custom-call(f32[2,4,8,8]{3,2,1,0:T(8,128)} %drive_hbm.1, s32[8,8]{1,0:T(8,128)} %flag_hbm.1, s32[8,8]{1,0:T(8,128)} %port_hbm.1, f32[2,8,1024]{2,1,0:T(8,128)} %feed_hbm.1, ...), custom_call_target="tpu_custom_call" | custom-call | tf_op jit(solution)/shard_map/pack/pallas_call | solution.py:421
  6.1 13.9 %all_to_all.10 = f32[32,8,128]{2,1,0:T(8,128)S(1)} all-to-all(f32[32,8,128]{2,1,0:T(8,128)S(1)} %get-tuple-element.9), channel_id=1, replica_groups={{240,256,272,288,304,320,336,352,368,384,400,416,432,448,464,480,496,0,..., dimensions={0} | all-to-all | bytes 262144 | tf_op jit(solution)/shard_map/all_to_all | solution.py:409
  20.0 0.9 %stencil.1 = (f32[416,128]{1,0:T(8,128)S(1)}, f32[16,256]{1,0:T(8,128)S(1)}) custom-call(f32[256,128]{1,0:T(8,128)S(1)} %bitcast.4, bf16[512,256]{1,0:T(8,128)(2,1)S(1)} %get-tuple-element.10.row_high_ref, bf16[512,256]{1,0:T(8,128)(2,1)S(1)} %get-tuple-element.11.row_low_ref), custom_call_target="tpu_custom_call" | custom-call | tf_op jit(solution)/shard_map/stencil/pallas_call | solution.py:443
  21.0 16.5 %all_to_all.11 = f32[16,13,2,128]{3,2,1,0:T(2,128)S(1)} all-to-all(f32[16,13,2,128]{3,2,1,0:T(2,128)S(1)} %bitcast.5), channel_id=1, replica_groups={{14,15,0,1,2,3,4,5,6,7,8,9,10,11,12,13},{30,31,16,17,18,19,20,21,22,23,..., dimensions={0} | all-to-all | bytes 425984 | tf_op jit(solution)/shard_map/all_to_all | solution.py:409
  37.4 1.0 %pattern.1 = (f32[2,4,8,8]{3,2,1,0:T(8,128)}, f32[2,4,32,32]{3,2,1,0:T(8,128)}) custom-call(f32[416,128]{1,0:T(8,128)S(1)} %bitcast.3, f32[16,256]{1,0:T(8,128)S(1)} %get-tuple-element.13.own_ref, bf16[64,416]{1,0:T(8,128)(2,1)S(1)} %get-tuple-element.14.col_high_ref, bf16[64,416]{1,0:T(8,128)(2,1)S(1)} %get-tuple-element.15.col_low_ref), custom_call_target="tpu_custom_call" | custom-call | tf_op jit(solution)/shard_map/pattern/pallas_call | solution.py:450

commit v8 on v7

--- a/solution.py
+++ b/solution.py
@@ -17,7 +17,8 @@
 WIDE = 12
 LANES = 128
 ROW_ORDER = tuple((15 + k) % 32 for k in range(32))
-COL_ORDER = tuple((14 + k) % 16 for k in range(16))
+COL_ORDER = (14, 4, 5, 7, 6, 0, 1, 3, 8, 9, 11, 2, 10, 12, 13, 15)
+MAKERS = (5, 1, 2, 3, 16, 17, 18, 19)
 PIECE = 26
 USED = 72
 
@@ -221,7 +222,11 @@
 
 
 def maker(row_at):
-    return row_at % 16 < 4, row_at % 4 + 4 * (row_at // 16)
+    makes, share = row_at < 0, row_at * 0
+    for k, member in enumerate(MAKERS):
+        makes = makes | (row_at == member)
+        share = jnp.where(row_at == member, k, share)
+    return makes, share
 
 
 def pack_kernel(
@@ -270,7 +275,7 @@
     none = jnp.zeros((8, rows), jnp.float32)
     north, south, north2, south2 = flag(r == 0), flag(r == rows - 1), flag(r == 1), flag(r == rows - 2)
     lane = lax.broadcasted_iota(jnp.int32, (BLOCK, LANES), 1)
-    makers = [slots[k % 4 + 16 * (k // 4)] for k in range(8)]
+    makers = [slots[k] for k in MAKERS]
     parts = [cells_ref[k : k + BLOCK, :] for k in makers]
     firsts = [jnp.where(lane < SHARE, pltpu.roll(part, LANES - USED, axis=1), 0.0) for part in parts[0::2]]
     seconds = [

time: 38.7 us -> 39.2 us (1.013)
  the two profiles are of different devices: /device:TPU:14 before, /device:TPU:8 now
where the time goes in v8:
time: 39.2 us; the launch traced here: 38.9 us
  blocking collectives  30.8 us (79%)
  Pallas kernels  7.46 us (19%)
  between operations  0.65 us (2%)
    all_to_all x2, blocking collectives, exchange(): return lax.all_to_all(pieces, axis, 0, 0, axis_index_groups=[list(order)])  30.8 us
    pallas_call x1, Pallas kernels, body(): call(functools.partial(pack_kernel, place, rows, cols), (pltpu.VMEM((row_...  5.51 us
    pallas_call x1, Pallas kernels, body(): call(functools.partial(pattern_kernel, place, col_blocks), (shape((2, STA...  1.03 us
    pallas_call x1, Pallas kernels, body(): call(functools.partial(stencil_kernel, place, rows, cols), (shape((col_bl...  0.93 us

profile of v8, /device:TPU:8, one launch (start us, length us, event | category | flops | bytes accessed | tf_op | source)
XLA Modules:
  0.0 38.9 jit_solution(3544201273562907207)
XLA Ops:
  0.6 5.5 %pack.1 = (f32[32,8,128]{2,1,0:T(8,128)S(1)}, bf16[512,256]{1,0:T(8,128)(2,1)S(1)}, bf16[512,256]{1,0:T(8,128)(2,1)S(1)}, bf16[64,416]{1,0:T(8,128)(2,1)S(1)}, bf16[64,416]{1,0:T(8,128)(2,1)S(1)}) custom-call(f32[2,4,8,8]{3,2,1,0:T(8,128)} %drive_hbm.1, s32[8,8]{1,0:T(8,128)} %flag_hbm.1, s32[8,8]{1,0:T(8,128)} %port_hbm.1, f32[2,8,1024]{2,1,0:T(8,128)} %feed_hbm.1, ...), custom_call_target="tpu_custom_call" | custom-call | tf_op jit(solution)/shard_map/pack/pallas_call | solution.py:426
  6.1 14.1 %all_to_all.10 = f32[32,8,128]{2,1,0:T(8,128)S(1)} all-to-all(f32[32,8,128]{2,1,0:T(8,128)S(1)} %get-tuple-element.9), channel_id=1, replica_groups={{240,256,272,288,304,320,336,352,368,384,400,416,432,448,464,480,496,0,..., dimensions={0} | all-to-all | bytes 262144 | tf_op jit(solution)/shard_map/all_to_all | solution.py:414
  20.3 0.9 %stencil.1 = (f32[416,128]{1,0:T(8,128)S(1)}, f32[16,256]{1,0:T(8,128)S(1)}) custom-call(f32[256,128]{1,0:T(8,128)S(1)} %bitcast.4, bf16[512,256]{1,0:T(8,128)(2,1)S(1)} %get-tuple-element.10.row_high_ref, bf16[512,256]{1,0:T(8,128)(2,1)S(1)} %get-tuple-element.11.row_low_ref), custom_call_target="tpu_custom_call" | custom-call | tf_op jit(solution)/shard_map/stencil/pallas_call | solution.py:448
  21.2 16.6 %all_to_all.11 = f32[16,13,2,128]{3,2,1,0:T(2,128)S(1)} all-to-all(f32[16,13,2,128]{3,2,1,0:T(2,128)S(1)} %bitcast.5), channel_id=1, replica_groups={{14,4,5,7,6,0,1,3,8,9,11,2,10,12,13,15},{30,20,21,23,22,16,17,19,24,25,..., dimensions={0} | all-to-all | bytes 425984 | tf_op jit(solution)/shard_map/all_to_all | solution.py:414
  37.8 1.0 %pattern.1 = (f32[2,4,8,8]{3,2,1,0:T(8,128)}, f32[2,4,32,32]{3,2,1,0:T(8,128)}) custom-call(f32[416,128]{1,0:T(8,128)S(1)} %bitcast.3, f32[16,256]{1,0:T(8,128)S(1)} %get-tuple-element.13.own_ref, bf16[64,416]{1,0:T(8,128)(2,1)S(1)} %get-tuple-element.14.col_high_ref, bf16[64,416]{1,0:T(8,128)(2,1)S(1)} %get-tuple-element.15.col_low_ref), custom_call_target="tpu_custom_call" | custom-call | tf_op jit(solution)/shard_map/pattern/pallas_call | solution.py:455

commit v9 on v7

--- a/solution.py
+++ b/solution.py
@@ -356,7 +356,7 @@
         out_ref[i * 4 * PIECE : (i + 1) * 4 * PIECE, :] = four
 
 
-def pattern_kernel(place, blocks, got_ref, own_ref, col_high_ref, col_low_ref, currents_ref, far_ref):
+def pattern_kernel(place, blocks, got_ref, own_ref, col_high_ref, col_low_ref, currents_hbm, far_hbm, currents_ref, far_ref, sems):
     _, col_at = place()
     samples = OVER * BLOCK
     far = dot3((col_high_ref[...], col_low_ref[...]), halves(got_ref[...]))
@@ -380,11 +380,15 @@
         ]
     stacked.append(jnp.zeros((LANES - 2 * samples - 2 * BLOCK, LANES), jnp.float32))
     flat = jnp.concatenate(stacked, axis=0).T
+    copies = []
     for x in range(2):
         at = 2 * samples + x * BLOCK
         for s in range(STATES):
             far_ref[x, s] = flat[s * samples : (s + 1) * samples, x * samples : (x + 1) * samples]
             currents_ref[x, s] = flat[s * samples : s * samples + BLOCK, at : at + BLOCK]
+        copies += fetch(sems.at[x], (far_ref.at[x], far_hbm.at[x]), (currents_ref.at[x], currents_hbm.at[x]))
+    for copy in copies:
+        copy.wait()
 
 
 def spot():
@@ -450,6 +454,12 @@
     return call(
         functools.partial(pattern_kernel, place, col_blocks),
         (shape((2, STATES, BLOCK, BLOCK), f32), shape((2, STATES, samples, samples), f32)),
+        scratch=[
+            pltpu.VMEM((2, STATES, BLOCK, BLOCK), f32),
+            pltpu.VMEM((2, STATES, samples, samples), f32),
+            pltpu.SemaphoreType.DMA((2, 2)),
+        ],
+        out_specs=(HBM, HBM),
         name="pattern",
     )(got.reshape(col_blocks * PIECE, LANES), own, col_high, col_low)
 

time: 38.7 us -> 38.7 us (level)
  no operation moved by 1% of the time
where the time goes in v9:
time: 38.7 us; the launch traced here: 38.5 us
  blocking collectives  30.4 us (79%)
  Pallas kernels  7.47 us (19%)
  between operations  0.65 us (2%)
    all_to_all x2, blocking collectives, exchange(): return lax.all_to_all(pieces, axis, 0, 0, axis_index_groups=[list(order)])  30.4 us
    pallas_call x1, Pallas kernels, body(): call(functools.partial(pack_kernel, place, rows, cols), (pltpu.VMEM((row_...  5.51 us
    pallas_call x1, Pallas kernels, body(): call(functools.partial(pattern_kernel, place, col_blocks), (shape((2, STA...  1.03 us
    pallas_call x1, Pallas kernels, body(): call(functools.partial(stencil_kernel, place, rows, cols), (shape((col_bl...  0.93 us

profile of v9, /device:TPU:14, one launch (start us, length us, event | category | flops | bytes accessed | tf_op | source)
XLA Modules:
  0.0 38.5 jit_solution(5350400040918327480)
XLA Ops:
  0.6 5.5 %pack.1 = (f32[32,8,128]{2,1,0:T(8,128)S(1)}, bf16[512,256]{1,0:T(8,128)(2,1)S(1)}, bf16[512,256]{1,0:T(8,128)(2,1)S(1)}, bf16[64,416]{1,0:T(8,128)(2,1)S(1)}, bf16[64,416]{1,0:T(8,128)(2,1)S(1)}) custom-call(f32[2,4,8,8]{3,2,1,0:T(8,128)} %drive_hbm.1, s32[8,8]{1,0:T(8,128)} %flag_hbm.1, s32[8,8]{1,0:T(8,128)} %port_hbm.1, f32[2,8,1024]{2,1,0:T(8,128)} %feed_hbm.1, ...), custom_call_target="tpu_custom_call" | custom-call | tf_op jit(solution)/shard_map/pack/pallas_call | solution.py:425
  6.1 13.9 %all_to_all.10 = f32[32,8,128]{2,1,0:T(8,128)S(1)} all-to-all(f32[32,8,128]{2,1,0:T(8,128)S(1)} %get-tuple-element.9), channel_id=1, replica_groups={{240,256,272,288,304,320,336,352,368,384,400,416,432,448,464,480,496,0,..., dimensions={0} | all-to-all | bytes 262144 | tf_op jit(solution)/shard_map/all_to_all | solution.py:413
  20.0 0.9 %stencil.1 = (f32[416,128]{1,0:T(8,128)S(1)}, f32[16,256]{1,0:T(8,128)S(1)}) custom-call(f32[256,128]{1,0:T(8,128)S(1)} %bitcast.4, bf16[512,256]{1,0:T(8,128)(2,1)S(1)} %get-tuple-element.10.row_high_ref, bf16[512,256]{1,0:T(8,128)(2,1)S(1)} %get-tuple-element.11.row_low_ref), custom_call_target="tpu_custom_call" | custom-call | tf_op jit(solution)/shard_map/stencil/pallas_call | solution.py:447
  21.0 16.5 %all_to_all.11 = f32[16,13,2,128]{3,2,1,0:T(2,128)S(1)} all-to-all(f32[16,13,2,128]{3,2,1,0:T(2,128)S(1)} %bitcast.5), channel_id=1, replica_groups={{14,15,0,1,2,3,4,5,6,7,8,9,10,11,12,13},{30,31,16,17,18,19,20,21,22,23,..., dimensions={0} | all-to-all | bytes 425984 | tf_op jit(solution)/shard_map/all_to_all | solution.py:413
  37.4 1.0 %pattern.1 = (f32[2,4,8,8]{3,2,1,0:T(8,128)}, f32[2,4,32,32]{3,2,1,0:T(8,128)}) custom-call(f32[416,128]{1,0:T(8,128)S(1)} %bitcast.3, f32[16,256]{1,0:T(8,128)S(1)} %get-tuple-element.13.own_ref, bf16[64,416]{1,0:T(8,128)(2,1)S(1)} %get-tuple-element.14.col_high_ref, bf16[64,416]{1,0:T(8,128)(2,1)S(1)} %get-tuple-element.15.col_low_ref), custom_call_target="tpu_custom_call" | custom-call | tf_op jit(solution)/shard_map/pattern/pallas_call | solution.py:454
